TPU v7x, 32 devices: a whole 2x2x4 slice. The times are simulated.
32 devices in a mesh: seq: 4 (over y, x), own: 8 (over z, core).
Axes of the slice: x: 2, y: 2, z: 4, core: 2. Of those that a mesh axis runs over, the one named last changes fastest.
Arguments:
- queries: bfloat16 [8, 512, 1024], P('own', 'seq'), may hold values from -6 to 6
- keys: bfloat16 [8, 512, 1024], P('own', 'seq'), may hold values from -6 to 6
- values: bfloat16 [8, 512, 1024], P('own', 'seq'), may hold values from -6 to 6
- gates: bfloat16 [8, 512, 1024], P('own', 'seq'), may hold values from -6 to 6
- lengths: int32 [8, 4], P('own'), may hold values from 1 to 256, 512 in all within a row
- gain: float32 [1024], replicated, may hold values from 0.1 to 1.9
- grad_out: bfloat16 [8, 512, 1024], P('own', 'seq'), may hold values from -6 to 6
Outputs:
- output: bfloat16 [8, 512, 1024], P('own', 'seq')
- grad_queries: bfloat16 [8, 512, 1024], P('own', 'seq')
- grad_keys: bfloat16 [8, 512, 1024], P('own', 'seq')
- grad_values: bfloat16 [8, 512, 1024], P('own', 'seq')
- grad_gates: bfloat16 [8, 512, 1024], P('own', 'seq')
- grad_gain: float32 [1024], replicated
Inputs may be any that keep to these rules, and one draw needn't show every extreme that they name: Each group's 4 lengths sum to 512; in every group the longest is exactly 256.
All inputs are finite; a program needn't handle non-finite values.
Results may differ from a plain program's by a relative error of at most 0.0058.
Values may be sent and summed in bfloat16 or wider, within the bound.
A program may use at most 128 MiB of HBM per device.

v0:
```python
import math

import jax
import jax.numpy as jnp
from jax import lax
from jax.sharding import PartitionSpec as P

H = 8


def shifted(array, axis, by):
    length = lax.axis_size(axis)
    pairs = [(i, i + by) for i in range(length) if 0 <= i + by < length]
    return lax.ppermute(array, axis, pairs)


def positions_info(pos, lens):
    ends = jnp.cumsum(lens)
    seg = jnp.sum((pos[:, None] >= ends[None, :]).astype(jnp.int32), axis=1)
    users = jnp.arange(lens.shape[0], dtype=jnp.int32)
    span = jnp.sum(jnp.where(seg[:, None] == users[None, :], lens[None, :], 0), axis=1)
    return (seg, 1.0 / jnp.maximum(span, 1).astype(jnp.float32))


def pair_weight(row_pos, row_seg, row_inverse, col_pos, col_seg):
    allowed = (row_seg[:, None] == col_seg[None, :]) & (col_pos[None, :] <= row_pos[:, None])
    allowed = allowed & (col_pos[None, :] >= 0) & (row_pos[:, None] >= 0)
    return jnp.where(allowed, row_inverse[:, None], jnp.float32(0.0))


def silu_slope(scores):
    sig = jax.nn.sigmoid(scores)
    return sig * (1.0 + scores * (1.0 - sig))


def per_device(queries, keys, values, gates, lengths, gain, grad_out):
    rows, width = (queries.shape[1], queries.shape[2])
    head_size = width // H
    scale = 1.0 / math.sqrt(head_size)
    lens = lengths[0]
    seq_count = lax.axis_size("seq")
    longest = rows * seq_count // 2
    reach = min(seq_count - 1, (longest - 1) // rows + 1)
    first = lax.axis_index("seq") * rows
    my_pos = first + jnp.arange(rows, dtype=jnp.int32)
    my_seg, my_inverse = positions_info(my_pos, lens)
    q3 = queries[0].reshape(rows, H, head_size)
    k3 = keys[0].reshape(rows, H, head_size)
    v3 = values[0].reshape(rows, H, head_size)

    def piece_info(start, count):
        col_pos = start + jnp.arange(count, dtype=jnp.int32)
        col_seg, col_inverse = positions_info(col_pos, lens)
        return (col_pos, col_seg, col_inverse)

    key_all, value_all = (
        lax.all_gather(keys, "seq", axis=1, tiled=True),
        lax.all_gather(values, "seq", axis=1, tiled=True),
    )
    total = key_all.shape[1]
    ka3 = key_all[0].reshape(total, H, head_size)
    va3 = value_all[0].reshape(total, H, head_size)
    col_pos, col_seg, col_inverse = piece_info(0, total)
    weight = pair_weight(my_pos, my_seg, my_inverse, col_pos, col_seg)
    scores = jnp.einsum("thd,shd->hts", q3, ka3, preferred_element_type=jnp.float32) * scale
    probs = (jax.nn.silu(scores) * weight[None]).astype(jnp.bfloat16)
    attended = jnp.einsum("hts,shd->thd", probs, va3, preferred_element_type=jnp.float32)
    attended = attended.reshape(rows, width)
    center = attended - jnp.mean(attended, axis=1, keepdims=True)
    rstd = lax.rsqrt(jnp.mean(center * center, axis=1, keepdims=True) + 1e-05)
    normed = center * rstd
    gate_f = gates[0].astype(jnp.float32)
    grad_f = grad_out[0].astype(jnp.float32)
    output = (normed * gain[None, :] * gate_f).astype(jnp.bfloat16)
    grad_gate = (grad_f * normed * gain[None, :]).astype(jnp.bfloat16)
    gain_part = jnp.sum(grad_f * gate_f * normed, axis=0)
    dnorm = grad_f * gate_f * gain[None, :]
    grad_att = rstd * (
        dnorm
        - jnp.mean(dnorm, axis=1, keepdims=True)
        - normed * jnp.mean(dnorm * normed, axis=1, keepdims=True)
    )
    grad_att = grad_att.astype(jnp.bfloat16)
    ga3 = grad_att.reshape(rows, H, head_size)
    grad_probs = jnp.einsum("thd,shd->hts", ga3, va3, preferred_element_type=jnp.float32)
    grad_scores = (grad_probs * weight[None] * silu_slope(scores)).astype(jnp.bfloat16)
    result = jnp.einsum("hts,shd->thd", grad_scores, ka3, preferred_element_type=jnp.float32)
    grad_q = (result * scale).reshape(rows, width).astype(jnp.bfloat16)
    query_list = [queries]
    grad_list = [grad_att[None]]
    for ahead in range(1, reach + 1):
        query_piece, grad_piece = shifted((queries, grad_att[None]), "seq", -ahead)
        query_list.append(query_piece)
        grad_list.append(grad_piece)
    query_block = jnp.concatenate(query_list, axis=1)
    grad_block = jnp.concatenate(grad_list, axis=1)
    count = query_block.shape[1]
    qp3 = query_block[0].reshape(count, H, head_size)
    gp3 = grad_block[0].reshape(count, H, head_size)
    row_pos, row_seg, row_inverse = piece_info(first, count)
    weight_piece = pair_weight(row_pos, row_seg, row_inverse, my_pos, my_seg)
    scores_piece = jnp.einsum("phd,khd->hpk", qp3, k3, preferred_element_type=jnp.float32) * scale
    probs_piece = (jax.nn.silu(scores_piece) * weight_piece[None]).astype(jnp.bfloat16)
    grad_probs = jnp.einsum("phd,khd->hpk", gp3, v3, preferred_element_type=jnp.float32)
    grad_scores = (grad_probs * weight_piece[None] * silu_slope(scores_piece)).astype(jnp.bfloat16)
    key_sum = jnp.einsum("hpk,phd->khd", grad_scores, qp3, preferred_element_type=jnp.float32)
    value_sum = jnp.einsum("hpk,phd->khd", probs_piece, gp3, preferred_element_type=jnp.float32)
    key_sum, value_sum = (key_sum, value_sum)
    grad_k = (key_sum * scale).reshape(rows, width).astype(jnp.bfloat16)
    grad_v = value_sum.reshape(rows, width).astype(jnp.bfloat16)
    grad_gain = lax.psum(gain_part, ("seq", "own"))
    return (output[None], grad_q[None], grad_k[None], grad_v[None], grad_gate[None], grad_gain)


def solution(mesh):
    in_specs = (
        P("own", "seq", None),
        P("own", "seq", None),
        P("own", "seq", None),
        P("own", "seq", None),
        P("own", None),
        P(),
        P("own", "seq", None),
    )
    out_specs = (
        P("own", "seq", None),
        P("own", "seq", None),
        P("own", "seq", None),
        P("own", "seq", None),
        P("own", "seq", None),
        P(),
    )
    return jax.shard_map(
        per_device, mesh=mesh, in_specs=in_specs, out_specs=out_specs, check_vma=False
    )
```

profile of v0, /device:TPU:2, one launch (start us, length us, event | category | flops | bytes accessed | tf_op | source)
XLA Modules:
  0.0 151.2 jit_solution(6874336116803942129)
XLA Ops:
  7.2 0.0 copy-start
  7.2 0.0 all-gather.3.cloned.1.call-start
  7.3 1.9 %copy.68 = bf16[1,128,1024]{1,2,0:T(8,128)(2,1)} copy(bf16[1,128,1024]{2,1,0:T(8,128)(2,1)} %param.8) | data formatting | bytes 524288 | tf_op args[1]
  9.1 0.0 all-gather.3.cloned.1.call-update
  9.2 0.0 copy-start.2
  9.2 0.0 all-gather.5.cloned.1.call-start
  9.2 1.2 copy.78
  10.4 1.3 collective-permute-start.1
  11.7 1.9 %collective-permute-start = (bf16[1,128,1024]{1,2,0:T(8,128)(2,1)S(1)}, bf16[1,128,1024]{1,2,0:T(8,128)(2,1)S(1)}, u32[]{:S(2)}, u32[]{:S(2)}) collective-permute-start(bf16[1,128,1024]{1,2,0:T(8,128)(2,1)S(1)} %copy.78), channel_id=1, source_target_pairs={{8,0},{16,8},{24,16},{9,1},{17,9},{25,17},{10,2},{18,10},{26,18},{... | collective-permute-start | bytes 786440 | tf_op jit(solution)/shard_map/ppermute | solution.py:14
  13.6 0.0 all-gather.5.cloned.1.call-update
  13.7 0.2 reduce-window.8
  13.9 0.1 convert_reduce_fusion.2
  13.9 0.1 select_reduce_fusion.1
  14.0 0.1 convert_reduce_fusion.1
  14.1 0.1 select_reduce_fusion
  14.2 1.0 and_select_fusion
  15.2 0.1 convert_reduce_fusion
  15.3 0.2 copy.73
  15.5 0.2 copy.72
  15.8 0.8 copy.100
  16.5 0.8 fusion.33
  17.4 11.4 %collective-permute-done.1 = bf16[1,128,1024]{1,2,0:T(8,128)(2,1)S(1)} collective-permute-done((bf16[1,128,1024]{1,2,0:T(8,128)(2,1)S(1)}, bf16[1,128,1024]{1,2,0:T(8,128)(2,1)S(1)}, u32[]{:S(2)}, u32[]{:S(2)}) %collective-permute-start.1) | collective-permute-done | bytes 262176 | tf_op jit(solution)/shard_map/ppermute | solution.py:14
  28.7 0.1 pad_maximum_fusion
  28.9 0.4 convolution_multiply_fusion
  29.3 12.4 %all-gather.3.cloned.1.call-done = bf16[1,512,1024]{1,2,0:T(8,128)(2,1)} async-done(((bf16[1,128,1024]{1,2,0:T(8,128)(2,1)}), bf16[1,512,1024]{1,2,0:T(8,128)(2,1)}) %all-gather.3.cloned.1.call-update) | async-done | bytes 1048592 | tf_op jit(solution)/shard_map/all_gather | solution.py:57
  41.7 3.0 %fusion.19 = f32[8,128,512]{2,1,0:T(8,128)} fusion(bf16[512,8,128]{0,2,1:T(8,128)(2,1)} %bitcast.77, bf16[128,8,128]{2,1,0:T(8,128)(2,1)S(1)} %bitcast.85), kind=kOutput, calls=%fused_computation.42 | convolution fusion | flops 134217728 | bytes 3407872 | tf_op jit(solution)/shard_map/thd,shd->hts/dot_general | solution.py:65
  44.7 25.5 %all-gather.5.cloned.1.call-done = bf16[1,512,1024]{2,1,0:T(8,128)(2,1)} async-done(((bf16[1,128,1024]{2,1,0:T(8,128)(2,1)}), bf16[1,512,1024]{2,1,0:T(8,128)(2,1)}) %all-gather.5.cloned.1.call-update) | async-done | bytes 1048592 | tf_op jit(solution)/shard_map/all_gather | solution.py:58
  70.2 2.3 %copy.71 = bf16[1,512,1024]{1,2,0:T(8,128)(2,1)} copy(bf16[1,512,1024]{2,1,0:T(8,128)(2,1)} %all-gather.5.cloned.1.call-done) | data formatting | bytes 2097152 | tf_op jit(solution)/shard_map/all_gather | solution.py:58
  72.5 2.9 %fusion.43 = (f32[128]{0:T(128)S(1)}, f32[8,128,128]{1,2,0:T(8,128)S(1)}) fusion(bf16[512,8,128]{0,2,1:T(8,128)(2,1)} %bitcast.79, f32[8,128,512]{2,1,0:T(8,128)} %fusion.19, f32[128,512]{1,0:T(8,128)} %fusion.33), kind=kOutput, calls=%fused_computation.80 | convolution fusion | flops 138018688 | bytes 3932672 | tf_op jit(solution)/shard_map/hts,shd->thd/dot_general | solution.py:67
  75.4 0.2 multiply_reduce_fusion.1
  75.5 0.4 fusion.14
  75.9 1.4 fusion.11
  77.3 1.3 collective-permute-start.3
  78.6 2.5 %collective-permute-start.2 = (bf16[1,128,1024]{1,2,0:T(8,128)(2,1)}, bf16[1,128,1024]{1,2,0:T(8,128)(2,1)}, u32[]{:S(2)}, u32[]{:S(2)}) collective-permute-start(bf16[1,128,1024]{1,2,0:T(8,128)(2,1)} %get-tuple-element.34), channel_id=1, source_target_pairs={{8,0},{16,8},{24,16},{9,1},{17,9},{25,17},{10,2},{18,10},{26,18},{... | collective-permute-start | bytes 786440 | tf_op jit(solution)/shard_map/ppermute | solution.py:14
  81.1 0.0 copy-start.4
  81.1 4.8 %fusion.1 = bf16[8,128,128]{1,2,0:T(8,128)(2,1)} fusion(bf16[512,8,128]{0,2,1:T(8,128)(2,1)} %bitcast.78, f32[8,128,512]{2,1,0:T(8,128)} %fusion.19, bf16[512,8,128]{0,2,1:T(8,128)(2,1)} %bitcast.80, f32[128,512]{1,0:T(8,128)} %fusion.33, f32[128,8,128]{0,2,1:T(8,128)} %bitcast.86, f32[8,128,128]{1,2,0:T(8,128)S(1)} %get-tuple-element.38, ...), kind=kOutput, calls=%fused_computation.11 | convolution fusion | flops 275513344 | bytes 5773312 | tf_op jit(solution)/shard_map/hts,shd->thd/dot_general | solution.py:87
  85.9 0.8 copy.88
  86.7 1.8 %copy.89 = bf16[1,128,1024]{2,1,0:T(8,128)(2,1)} copy(bf16[1,128,1024]{1,2,0:T(8,128)(2,1)} %bitcast.88) | data formatting | bytes 524288
  88.5 1.1 copy.79
  89.7 0.9 copy.92
  90.5 43.6 %psum.7 = f32[1024]{0:T(1024)} all-reduce(f32[1024]{0:T(1024)S(1)} %get-tuple-element.30), channel_id=1, replica_groups=mesh['seq'=4,'own'=8] {'seq','own'}, use_global_device_ids=true, to_apply=%region_11.12 | all-reduce | flops 1024 | bytes 8192 | tf_op jit(solution)/shard_map/psum | solution.py:111
  134.1 1.1 copy.81
  135.2 1.8 %copy.80 = bf16[128,8,128]{2,0,1:T(8,128)(2,1)} copy(bf16[128,8,128]{0,2,1:T(8,128)(2,1)} %bitcast.15) | data formatting | bytes 524288 | tf_op jit(solution)/shard_map/concatenate | solution.py:96
  137.0 1.8 %convolution_convert_fusion = bf16[8,128,128]{2,1,0:T(8,128)(2,1)S(1)} fusion(f32[8,384,128]{2,1,0:T(8,128)S(1)} %convolution_multiply_fusion, f32[384,128]{1,0:T(8,128)} %and_select_fusion, bf16[128,8,128]{2,0,1:T(8,128)(2,1)S(1)} %copy.81, bf16[128,8,128]{2,0,1:T(8,128)(2,1)} %copy.80, bf16[128,8,128]{2,0,1:T(8,128)(2,1)S(1)} %copy.79), kind=kOutput, calls=%fused_computation.10 | convolution fusion | flops 105512960 | bytes 2818048 | tf_op jit(solution)/shard_map/hpk,phd->khd/dot_general | solution.py:107
  138.8 2.7 %fusion.2 = bf16[128,8,128]{2,0,1:T(8,128)(2,1)} fusion(bf16[384,8,128]{0,2,1:T(8,128)(2,1)S(1)} %bitcast.75, f32[8,384,128]{2,1,0:T(8,128)S(1)} %convolution_multiply_fusion, f32[384,128]{1,0:T(8,128)} %and_select_fusion, bf16[128,8,128]{2,0,1:T(8,128)(2,1)S(1)} %copy.81, bf16[128,8,128]{2,0,1:T(8,128)(2,1)} %copy.80, bf16[128,8,128]{2,0,1:T(8,128)(2,1)S(1)} %copy.79, ...), kind=kOutput, calls=%fused_computation.12 | convolution fusion | flops 207880192 | bytes 3866624 | tf_op jit(solution)/shard_map/hpk,phd->khd/dot_general | solution.py:106
  141.6 1.1 copy.86
  142.7 0.9 copy.90
  143.6 0.8 copy.91
  (31 shorter events, 0.2 us)
Async XLA Ops:
  7.2 8.3 %copy-start = (bf16[1,128,1024]{2,1,0:T(8,128)(2,1)S(1)}, bf16[1,128,1024]{2,1,0:T(8,128)(2,1)}, u32[]{:S(2)}) copy-start(bf16[1,128,1024]{2,1,0:T(8,128)(2,1)} %param.7) | copy-start | bytes 786436
  7.2 8.5 %copy-start.1 = (bf16[1,128,1024]{2,1,0:T(8,128)(2,1)S(1)}, bf16[1,128,1024]{2,1,0:T(8,128)(2,1)}, u32[]{:S(2)}) copy-start(bf16[1,128,1024]{2,1,0:T(8,128)(2,1)} %param.8) | copy-start | bytes 786436
  7.2 6.5 %copy-start.9 = (s32[1,4]{1,0:T(1,128)S(1)}, s32[1,4]{1,0:T(1,128)}, u32[]{:S(2)}) copy-start(s32[1,4]{1,0:T(1,128)} %param.11) | copy-start | bytes 52
  7.2 8.1 %copy-start.5 = (bf16[1,128,1024]{2,1,0:T(8,128)(2,1)S(1)}, bf16[1,128,1024]{2,1,0:T(8,128)(2,1)}, u32[]{:S(2)}) copy-start(bf16[1,128,1024]{2,1,0:T(8,128)(2,1)} %param.13) | copy-start | bytes 786436
  7.2 8.3 %copy-start.6 = (bf16[1,128,1024]{2,1,0:T(8,128)(2,1)S(1)}, bf16[1,128,1024]{2,1,0:T(8,128)(2,1)}, u32[]{:S(2)}) copy-start(bf16[1,128,1024]{2,1,0:T(8,128)(2,1)} %param.10) | copy-start | bytes 786436
  7.2 34.5 %all-gather.3.cloned.1.call-start = ((), (), s32[]{:S(2)}) async-start(), calls=%async_computation | async-start | bytes 1310720 | tf_op jit(solution)/shard_map/all_gather | solution.py:57
  9.2 6.6 %copy-start.2 = (bf16[1,128,1024]{2,1,0:T(8,128)(2,1)S(1)}, bf16[1,128,1024]{2,1,0:T(8,128)(2,1)}, u32[]{:S(2)}) copy-start(bf16[1,128,1024]{2,1,0:T(8,128)(2,1)} %param.9) | copy-start | bytes 786436
  9.2 61.0 %all-gather.5.cloned.1.call-start = ((), (), s32[]{:S(2)}) async-start(), calls=%async_computation.1 | async-start | bytes 1310720 | tf_op jit(solution)/shard_map/all_gather | solution.py:58
  10.4 18.4 %collective-permute-start.1 = (bf16[1,128,1024]{1,2,0:T(8,128)(2,1)S(1)}, bf16[1,128,1024]{1,2,0:T(8,128)(2,1)S(1)}, u32[]{:S(2)}, u32[]{:S(2)}) collective-permute-start(bf16[1,128,1024]{1,2,0:T(8,128)(2,1)S(1)} %copy.78), channel_id=1, source_target_pairs={{16,0},{24,8},{17,1},{25,9},{18,2},{26,10},{19,3},{27,11},{20,4},{... | collective-permute-start | bytes 786440 | tf_op jit(solution)/shard_map/ppermute | solution.py:14
  11.7 17.1 %collective-permute-start = (bf16[1,128,1024]{1,2,0:T(8,128)(2,1)S(1)}, bf16[1,128,1024]{1,2,0:T(8,128)(2,1)S(1)}, u32[]{:S(2)}, u32[]{:S(2)}) collective-permute-start(bf16[1,128,1024]{1,2,0:T(8,128)(2,1)S(1)} %copy.78), channel_id=1, source_target_pairs={{8,0},{16,8},{24,16},{9,1},{17,9},{25,17},{10,2},{18,10},{26,18},{... | collective-permute-start | bytes 786440 | tf_op jit(solution)/shard_map/ppermute | solution.py:14
  72.5 3.0 %copy-start.8 = (f32[1024]{0:T(1024)S(1)}, f32[1024]{0:T(1024)}, u32[]{:S(2)}) copy-start(f32[1024]{0:T(1024)} %param.12) | copy-start | bytes 12292
  77.3 56.8 %collective-permute-start.3 = (bf16[1,128,1024]{1,2,0:T(8,128)(2,1)}, bf16[1,128,1024]{1,2,0:T(8,128)(2,1)}, u32[]{:S(2)}, u32[]{:S(2)}) collective-permute-start(bf16[1,128,1024]{1,2,0:T(8,128)(2,1)} %get-tuple-element.34), channel_id=1, source_target_pairs={{16,0},{24,8},{17,1},{25,9},{18,2},{26,10},{19,3},{27,11},{20,4},{... | collective-permute-start | bytes 786440 | tf_op jit(solution)/shard_map/ppermute | solution.py:14
  78.6 56.6 %collective-permute-start.2 = (bf16[1,128,1024]{1,2,0:T(8,128)(2,1)}, bf16[1,128,1024]{1,2,0:T(8,128)(2,1)}, u32[]{:S(2)}, u32[]{:S(2)}) collective-permute-start(bf16[1,128,1024]{1,2,0:T(8,128)(2,1)} %get-tuple-element.34), channel_id=1, source_target_pairs={{8,0},{16,8},{24,16},{9,1},{17,9},{25,17},{10,2},{18,10},{26,18},{... | collective-permute-start | bytes 786440 | tf_op jit(solution)/shard_map/ppermute | solution.py:14
  81.1 4.8 %copy-start.4 = (bf16[1,128,1024]{1,2,0:T(8,128)(2,1)S(1)}, bf16[1,128,1024]{1,2,0:T(8,128)(2,1)}, u32[]{:S(2)}) copy-start(bf16[1,128,1024]{1,2,0:T(8,128)(2,1)} %get-tuple-element.35) | copy-start | bytes 786436
  85.9 3.8 %copy-start.3 = (bf16[1,128,1024]{1,2,0:T(8,128)(2,1)S(1)}, bf16[1,128,1024]{1,2,0:T(8,128)(2,1)}, u32[]{:S(2)}) copy-start(bf16[1,128,1024]{1,2,0:T(8,128)(2,1)} %get-tuple-element.33) | copy-start | bytes 786436
  137.0 1.8 %copy-start.7 = (bf16[16,8,8,128]{3,2,1,0:T(8,128)(2,1)S(1)}, bf16[16,8,8,128]{3,2,1,0:T(8,128)(2,1)}, u32[]{:S(2)}) copy-start(bf16[16,8,8,128]{3,2,1,0:T(8,128)(2,1)} %copy.100) | copy-start | bytes 786436
Sparse Core Ops, SparseCore 0:
  10.5 31.1 all-gather.2
  43.5 26.6 all-gather.4
where the time goes:
time: 152 us; the launch traced here: 151 us
  waiting for transfers between devices  49.3 us (32%)
  blocking collectives  43.6 us (29%)
  local copies, waits for them, and re-layouts  16.9 us (11%)
  matrix products  15.6 us (10%)
  between operations  14.3 us (9%)
  starting transfers between devices  7.05 us (5%)
  other arithmetic  4.48 us (3%)
    psum x1, blocking collectives, per_device(): grad_gain = lax.psum(gain_part, ('seq', 'own'))  43.6 us
    all_gather x1, waiting for transfers between devices, per_device(): lax.all_gather(values, 'seq', axis=1, tiled=True)  25.5 us
    all_gather x1, waiting for transfers between devices, per_device(): lax.all_gather(keys, 'seq', axis=1, tiled=True)  12.4 us
    ppermute x4, waiting for transfers between devices, shifted(): return lax.ppermute(array, axis, pairs)  11.4 us
    unnamed x32, local copies, waits for them, and re-layouts  9.44 us
    ppermute x4, starting transfers between devices, shifted(): return lax.ppermute(array, axis, pairs)  6.97 us
    dot_general x1, matrix products, per_device(): jnp.einsum('hts,shd->thd', grad_scores, ka3, preferred_element_type=jnp.f...  4.76 us
    concatenate x3, local copies, waits for them, and re-layouts, per_device(): grad_block = jnp.concatenate(grad_list, axis=1)  4.03 us
  transfers between devices with their start and end apart: 6, of which 3 were waited for; matrix products, arithmetic and copies ran while one was open for 12% of the time, Pallas kernels for 0%

commit v1 on v0

v1 whole, which is shorter than its diff:
```python
import functools
import math

import jax
import jax.numpy as jnp
from jax import lax
from jax.experimental import pallas as pl
from jax.experimental.pallas import tpu as pltpu
from jax.sharding import PartitionSpec as P

H = 8
MESH = pl.DeviceIdType.MESH
K, V, Q, G = 0, 1, 2, 3


def dot_nt(a, b):
    return lax.dot_general(a, b, (((1,), (1,)), ((), ())), preferred_element_type=jnp.float32)


def dot_nn(a, b):
    return lax.dot_general(a, b, (((1,), (0,)), ((), ())), preferred_element_type=jnp.float32)


def silu_and_slope(scores):
    sig = 0.5 * jnp.tanh(0.5 * scores) + 0.5
    silu = scores * sig
    return silu, sig + silu * (1.0 - sig)


def kernel(
    n, m, reach, scale,
    lens_ref, gain_ref, q_hbm, k_hbm, v_hbm, gate_hbm, grad_hbm,
    out_hbm, gq_hbm, gk_hbm, gv_hbm, gg_hbm, ggain_ref,
    blocks, gate, grad, row_probs, row_slope, col_probs, col_slope,
    attended, gq_sum, gk_sum, gv_sum, results,
    part, seq_parts, total, own_parts,
    load_sem, store_sem, send_sem, recv_sem, seq_send, seq_recv, own_send, own_recv,
):
    me = lax.axis_index("seq")
    mine = lax.axis_index("own")
    rows, width = gate.shape
    head = width // H
    users = lens_ref.shape[1]
    hbm = {K: k_hbm, V: v_hbm, Q: q_hbm}

    def cols(h):
        return slice(h * head, (h + 1) * head)

    def steps(low, body):
        if reach <= 3:
            for d in range(low, reach + 1):
                body(d)
        else:
            pl.loop(low, reach + 1)(body)

    def load(i, src, dst):
        return pltpu.make_async_copy(src, dst, load_sem.at[i])

    loads = [
        load(0, q_hbm.at[0], blocks.at[Q, 0]),
        load(1, k_hbm.at[0], blocks.at[K, 0]),
        load(2, v_hbm.at[0], blocks.at[V, 0]),
        load(3, gate_hbm.at[0], gate),
        load(4, grad_hbm.at[0], grad),
    ]
    for copy in loads:
        copy.start()

    barrier = pltpu.get_barrier_semaphore()

    @pl.loop(1, n)
    def _(j):
        pl.semaphore_signal(barrier, 1, device_id={"seq": lax.rem(me + j, n)}, device_id_type=MESH)

    @pl.loop(1, m)
    def _(j):
        pl.semaphore_signal(barrier, 1, device_id={"own": lax.rem(mine + j, m)}, device_id_type=MESH)

    pl.semaphore_wait(barrier, n + m - 2)

    def send(what, d):
        peer = me + d if what in (K, V) else me - d
        src = blocks.at[G, 0] if what == G else hbm[what].at[0]
        return pltpu.make_async_remote_copy(
            src_ref=src, dst_ref=blocks.at[what, d],
            send_sem=send_sem.at[what, d], recv_sem=recv_sem.at[what, d],
            device_id={"seq": peer}, device_id_type=MESH,
        )

    def can_send(what, d):
        return me + d < n if what in (K, V) else me >= d

    def start(what):
        def body(d):
            @pl.when(can_send(what, d))
            def _():
                send(what, d).start()
        steps(1, body)

    def wait_sends(what):
        def body(d):
            @pl.when(can_send(what, d))
            def _():
                send(what, d).wait_send()
        steps(1, body)

    start(K)
    start(V)
    start(Q)

    def weight(row_block, col_block, row_dim):
        t = row_block * rows + lax.broadcasted_iota(jnp.int32, (rows, rows), row_dim)
        s = col_block * rows + lax.broadcasted_iota(jnp.int32, (rows, rows), 1 - row_dim)
        first = jnp.zeros_like(t)
        span = jnp.ones_like(t)
        end = jnp.int32(0)
        for u in range(users):
            begin, end = end, end + lens_ref[0, u]
            inside = (t >= begin) & (t < end)
            first = jnp.where(inside, begin, first)
            span = jnp.where(inside, lens_ref[0, u], span)
        inverse = 1.0 / span.astype(jnp.float32)
        return jnp.where((s >= first) & (s <= t), inverse, 0.0)

    for copy in loads[:3]:
        copy.wait()

    def row_scores(d):
        @pl.when(me >= d)
        def _():
            if not isinstance(d, int) or d > 0:
                send(K, d).wait_recv()
            w = weight(me, me - d, 0)
            for h in range(H):
                scores = dot_nt(blocks[Q, 0, :, cols(h)], blocks[K, d, :, cols(h)]) * scale
                silu, slope = silu_and_slope(scores)
                row_probs[d, h] = (silu * w).astype(jnp.bfloat16)
                row_slope[d, h] = slope * w

    def row_attend(d):
        @pl.when(me >= d)
        def _():
            send(V, d).wait_recv()
            for h in range(H):
                attended[:, cols(h)] += dot_nn(row_probs[d, h], blocks[V, d, :, cols(h)])

    row_scores(0)
    for h in range(H):
        attended[:, cols(h)] = dot_nn(row_probs[0, h], blocks[V, 0, :, cols(h)])
    steps(1, row_scores)
    steps(1, row_attend)

    for copy in loads[3:]:
        copy.wait()
    gain = gain_ref[...]
    step = 32 if rows % 32 == 0 else rows
    share = jnp.zeros((1, width), jnp.float32)
    for r in range(0, rows, step):
        at = slice(r, r + step)
        att = attended[at, :]
        center = att - jnp.mean(att, axis=1, keepdims=True)
        rstd = lax.rsqrt(jnp.mean(center * center, axis=1, keepdims=True) + 1e-05)
        normed = center * rstd
        gate_f = gate[at, :].astype(jnp.float32)
        grad_f = grad[at, :].astype(jnp.float32)
        scaled = normed * gain
        results[0, at, :] = (scaled * gate_f).astype(jnp.bfloat16)
        results[1, at, :] = (grad_f * scaled).astype(jnp.bfloat16)
        both = grad_f * gate_f
        share = share + jnp.sum(both * normed, axis=0, keepdims=True)
        dnorm = both * gain
        back = rstd * (
            dnorm
            - jnp.mean(dnorm, axis=1, keepdims=True)
            - normed * jnp.mean(dnorm * normed, axis=1, keepdims=True)
        )
        blocks[G, 0, at, :] = back.astype(jnp.bfloat16)
    start(G)
    part[...] = share

    def seq_share(j):
        return pltpu.make_async_remote_copy(
            src_ref=part, dst_ref=seq_parts.at[me],
            send_sem=seq_send.at[j], recv_sem=seq_recv.at[me],
            device_id={"seq": lax.rem(me + j, n)}, device_id_type=MESH,
        )

    def own_share(j):
        return pltpu.make_async_remote_copy(
            src_ref=total, dst_ref=own_parts.at[mine],
            send_sem=own_send.at[j], recv_sem=own_recv.at[mine],
            device_id={"own": lax.rem(mine + j, m)}, device_id_type=MESH,
        )

    pl.loop(1, n)(lambda j: seq_share(j).start())
    seq_parts[me] = share

    def store(i, dst):
        return pltpu.make_async_copy(results.at[i], dst.at[0], store_sem.at[i])

    stores = [store(i, dst) for i, dst in enumerate((out_hbm, gg_hbm, gq_hbm, gk_hbm, gv_hbm))]
    stores[0].start()
    stores[1].start()

    def row_back(d):
        @pl.when(me >= d)
        def _():
            for h in range(H):
                grad_probs = dot_nt(blocks[G, 0, :, cols(h)], blocks[V, d, :, cols(h)])
                grad_scores = (grad_probs * row_slope[d, h]).astype(jnp.bfloat16)
                term = dot_nn(grad_scores, blocks[K, d, :, cols(h)])
                if isinstance(d, int) and d == 0:
                    gq_sum[:, cols(h)] = term
                else:
                    gq_sum[:, cols(h)] += term

    row_back(0)
    steps(1, row_back)
    results[2] = (gq_sum[...] * scale).astype(jnp.bfloat16)
    stores[2].start()

    @pl.loop(1, n)
    def _(j):
        src = lax.rem(me + j, n)
        pltpu.make_async_remote_copy(
            src_ref=part, dst_ref=seq_parts.at[src],
            send_sem=seq_send.at[j], recv_sem=seq_recv.at[src],
            device_id={"seq": src}, device_id_type=MESH,
        ).wait_recv()

    group = seq_parts[0]
    for j in range(1, n):
        group = group + seq_parts[j]
    total[...] = group
    pl.loop(1, m)(lambda j: own_share(j).start())
    own_parts[mine] = group

    def col_scores(d):
        @pl.when(me + d < n)
        def _():
            if not isinstance(d, int) or d > 0:
                send(Q, d).wait_recv()
            w = weight(me + d, me, 1)
            for h in range(H):
                scores = dot_nt(blocks[K, 0, :, cols(h)], blocks[Q, d, :, cols(h)]) * scale
                silu, slope = silu_and_slope(scores)
                col_probs[d, h] = (silu * w).astype(jnp.bfloat16)
                col_slope[d, h] = slope * w

    def col_back(d):
        @pl.when(me + d < n)
        def _():
            own = isinstance(d, int) and d == 0
            if not own:
                send(G, d).wait_recv()
            for h in range(H):
                back = blocks[G, d, :, cols(h)]
                grad_probs = dot_nt(blocks[V, 0, :, cols(h)], back)
                grad_scores = (grad_probs * col_slope[d, h]).astype(jnp.bfloat16)
                key_term = dot_nn(grad_scores, blocks[Q, d, :, cols(h)])
                value_term = dot_nn(col_probs[d, h], back)
                if own:
                    gk_sum[:, cols(h)] = key_term
                    gv_sum[:, cols(h)] = value_term
                else:
                    gk_sum[:, cols(h)] += key_term
                    gv_sum[:, cols(h)] += value_term

    col_scores(0)
    steps(1, col_scores)
    col_back(0)
    steps(1, col_back)
    results[3] = (gk_sum[...] * scale).astype(jnp.bfloat16)
    results[4] = gv_sum[...].astype(jnp.bfloat16)
    stores[3].start()
    stores[4].start()

    @pl.loop(1, m)
    def _(j):
        src = lax.rem(mine + j, m)
        pltpu.make_async_remote_copy(
            src_ref=total, dst_ref=own_parts.at[src],
            send_sem=own_send.at[j], recv_sem=own_recv.at[src],
            device_id={"own": src}, device_id_type=MESH,
        ).wait_recv()

    whole = own_parts[0]
    for j in range(1, m):
        whole = whole + own_parts[j]
    ggain_ref[...] = whole

    for what in (K, V, Q, G):
        wait_sends(what)
    pl.loop(1, n)(lambda j: seq_share(j).wait_send())
    pl.loop(1, m)(lambda j: own_share(j).wait_send())
    for copy in stores:
        copy.wait()


def per_device(n, m, queries, keys, values, gates, lengths, gain, grad_out):
    rows, width = queries.shape[1], queries.shape[2]
    head = width // H
    reach = min(n - 1, (rows * n // 2 - 1) // rows + 1)
    slots = reach + 1
    any_spec = pl.BlockSpec(memory_space=pl.ANY)
    vmem = pl.BlockSpec(memory_space=pltpu.VMEM)
    block = jax.ShapeDtypeStruct(queries.shape, jnp.bfloat16)
    dma = pltpu.SemaphoreType.DMA
    outs = pl.pallas_call(
        functools.partial(kernel, n, m, reach, 1.0 / math.sqrt(head)),
        out_shape=[block] * 5 + [jax.ShapeDtypeStruct((1, width), jnp.float32)],
        in_specs=[pl.BlockSpec(memory_space=pltpu.SMEM), vmem] + [any_spec] * 5,
        out_specs=[any_spec] * 5 + [vmem],
        scratch_shapes=[
            pltpu.VMEM((4, slots, rows, width), jnp.bfloat16),
            pltpu.VMEM((rows, width), jnp.bfloat16),
            pltpu.VMEM((rows, width), jnp.bfloat16),
            pltpu.VMEM((slots, H, rows, rows), jnp.bfloat16),
            pltpu.VMEM((slots, H, rows, rows), jnp.float32),
            pltpu.VMEM((slots, H, rows, rows), jnp.bfloat16),
            pltpu.VMEM((slots, H, rows, rows), jnp.float32),
            pltpu.VMEM((rows, width), jnp.float32),
            pltpu.VMEM((rows, width), jnp.float32),
            pltpu.VMEM((rows, width), jnp.float32),
            pltpu.VMEM((rows, width), jnp.float32),
            pltpu.VMEM((5, rows, width), jnp.bfloat16),
            pltpu.VMEM((1, width), jnp.float32),
            pltpu.VMEM((n, 1, width), jnp.float32),
            pltpu.VMEM((1, width), jnp.float32),
            pltpu.VMEM((m, 1, width), jnp.float32),
            dma((5,)), dma((5,)), dma((4, slots)), dma((4, slots)),
            dma((n,)), dma((n,)), dma((m,)), dma((m,)),
        ],
        compiler_params=pltpu.CompilerParams(
            collective_id=0, has_side_effects=True, vmem_limit_bytes=44 * 1024 * 1024
        ),
        cost_estimate=pl.CostEstimate(
            flops=16 * slots * rows * rows * width, bytes_accessed=20 * rows * width, transcendentals=0
        ),
    )(lengths, gain.reshape(1, width), queries, keys, values, gates, grad_out)
    output, grad_q, grad_k, grad_v, grad_gate, grad_gain = outs
    return output, grad_q, grad_k, grad_v, grad_gate, grad_gain.reshape(width)


def solution(mesh):
    blocked = P("own", "seq", None)
    sizes = (mesh.shape["seq"], mesh.shape["own"])
    return jax.shard_map(
        functools.partial(per_device, *sizes),
        mesh=mesh,
        in_specs=(blocked, blocked, blocked, blocked, P("own", None), P(), blocked),
        out_specs=(blocked, blocked, blocked, blocked, blocked, P()),
        check_vma=False,
    )
```

time: 152 us -> 53.8 us (0.35)
  the two profiles are of different devices: /device:TPU:2 before, /device:TPU:0 now
where the time goes in v1:
time: 53.8 us; the launch traced here: 53.5 us
  Pallas kernels  42.6 us (79%)
  local copies, waits for them, and re-layouts  10.2 us (19%)
  between operations  0.66 us (1%)
    pallas_call x1, Pallas kernels, per_device(): pl.pallas_call(functools.partial(kernel, n, m, reach, 1.0 / math.sqrt(hea...  42.6 us
    unnamed x20, local copies, waits for them, and re-layouts  10.2 us

profile of v1, /device:TPU:0, one launch (start us, length us, event | category | flops | bytes accessed | tf_op | source)
XLA Modules:
  0.0 53.5 jit_solution(2371904064855277118)
XLA Ops:
  0.6 0.0 copy-start.6
  0.6 0.6 %copy-done.6 = s32[1,4]{1,0:T(1,128)S(1)} copy-done((s32[1,4]{1,0:T(1,128)S(1)}, s32[1,4]{1,0:T(1,128)}, u32[]{:S(2)}) %copy-start.6) | copy-done | bytes 40
  1.3 0.0 copy-start
  1.3 0.9 %copy-done = bf16[1,128,1024]{2,1,0:T(8,128)(2,1)S(1)} copy-done((bf16[1,128,1024]{2,1,0:T(8,128)(2,1)S(1)}, bf16[1,128,1024]{2,1,0:T(8,128)(2,1)}, u32[]{:S(2)}) %copy-start) | copy-done | bytes 262168
  2.2 0.0 copy-start.1
  2.2 0.9 %copy-done.1 = bf16[1,128,1024]{2,1,0:T(8,128)(2,1)S(1)} copy-done((bf16[1,128,1024]{2,1,0:T(8,128)(2,1)S(1)}, bf16[1,128,1024]{2,1,0:T(8,128)(2,1)}, u32[]{:S(2)}) %copy-start.1) | copy-done | bytes 262168
  3.2 0.0 copy-start.2
  3.2 0.9 %copy-done.2 = bf16[1,128,1024]{2,1,0:T(8,128)(2,1)S(1)} copy-done((bf16[1,128,1024]{2,1,0:T(8,128)(2,1)S(1)}, bf16[1,128,1024]{2,1,0:T(8,128)(2,1)}, u32[]{:S(2)}) %copy-start.2) | copy-done | bytes 262168
  4.1 0.0 copy-start.3
  4.1 0.9 %copy-done.3 = bf16[1,128,1024]{2,1,0:T(8,128)(2,1)S(1)} copy-done((bf16[1,128,1024]{2,1,0:T(8,128)(2,1)S(1)}, bf16[1,128,1024]{2,1,0:T(8,128)(2,1)}, u32[]{:S(2)}) %copy-start.3) | copy-done | bytes 262168
  5.1 0.0 copy-start.4
  5.1 0.9 %copy-done.4 = bf16[1,128,1024]{2,1,0:T(8,128)(2,1)S(1)} copy-done((bf16[1,128,1024]{2,1,0:T(8,128)(2,1)S(1)}, bf16[1,128,1024]{2,1,0:T(8,128)(2,1)}, u32[]{:S(2)}) %copy-start.4) | copy-done | bytes 262168
  6.0 0.0 copy-start.5
  6.0 0.7 %copy-done.5 = f32[1024]{0:T(1024)S(1)} copy-done((f32[1024]{0:T(1024)S(1)}, f32[1024]{0:T(1024)}, u32[]{:S(2)}) %copy-start.5) | copy-done | bytes 4120
  6.7 42.6 %shard_map.118 = (bf16[1,128,1024]{2,1,0:T(8,128)(2,1)S(1)}, bf16[1,128,1024]{2,1,0:T(8,128)(2,1)S(1)}, bf16[1,128,1024]{2,1,0:T(8,128)(2,1)S(1)}, bf16[1,128,10...) custom-call(s32[1,4]{1,0:T(1,128)S(1)} %copy-done.6, f32[1,1024]{1,0:T(1,128)S(1)} %bitcast.3, ...), custom_call_target="tpu_custom_call" | custom-call | flops 805306368 | bytes 2621440 | tf_op jit(solution)/shard_map/pallas_call | solution.py:309
  49.4 0.7 %copy.19 = bf16[1,128,1024]{2,1,0:T(8,128)(2,1)} copy(bf16[1,128,1024]{2,1,0:T(8,128)(2,1)S(1)} %get-tuple-element.24) | data formatting | bytes 524288
  50.1 0.7 %copy.20 = bf16[1,128,1024]{2,1,0:T(8,128)(2,1)} copy(bf16[1,128,1024]{2,1,0:T(8,128)(2,1)S(1)} %get-tuple-element.25) | data formatting | bytes 524288
  50.8 0.7 %copy.21 = bf16[1,128,1024]{2,1,0:T(8,128)(2,1)} copy(bf16[1,128,1024]{2,1,0:T(8,128)(2,1)S(1)} %get-tuple-element.26) | data formatting | bytes 524288
  51.5 0.7 %copy.22 = bf16[1,128,1024]{2,1,0:T(8,128)(2,1)} copy(bf16[1,128,1024]{2,1,0:T(8,128)(2,1)S(1)} %get-tuple-element.27) | data formatting | bytes 524288
  52.2 0.7 %copy.23 = bf16[1,128,1024]{2,1,0:T(8,128)(2,1)} copy(bf16[1,128,1024]{2,1,0:T(8,128)(2,1)S(1)} %get-tuple-element.28) | data formatting | bytes 524288
  52.9 0.6 %copy.24 = f32[1024]{0:T(1024)} copy(f32[1024]{0:T(1024)S(1)} %bitcast.2) | data formatting | bytes 8192
Async XLA Ops:
  0.6 0.7 %copy-start.6 = (s32[1,4]{1,0:T(1,128)S(1)}, s32[1,4]{1,0:T(1,128)}, u32[]{:S(2)}) copy-start(s32[1,4]{1,0:T(1,128)} %lens_ref.1) | copy-start | bytes 52
  1.3 0.9 %copy-start = (bf16[1,128,1024]{2,1,0:T(8,128)(2,1)S(1)}, bf16[1,128,1024]{2,1,0:T(8,128)(2,1)}, u32[]{:S(2)}) copy-start(bf16[1,128,1024]{2,1,0:T(8,128)(2,1)} %q_hbm.1) | copy-start | bytes 786436
  2.2 0.9 %copy-start.1 = (bf16[1,128,1024]{2,1,0:T(8,128)(2,1)S(1)}, bf16[1,128,1024]{2,1,0:T(8,128)(2,1)}, u32[]{:S(2)}) copy-start(bf16[1,128,1024]{2,1,0:T(8,128)(2,1)} %k_hbm.1) | copy-start | bytes 786436
  3.2 0.9 %copy-start.2 = (bf16[1,128,1024]{2,1,0:T(8,128)(2,1)S(1)}, bf16[1,128,1024]{2,1,0:T(8,128)(2,1)}, u32[]{:S(2)}) copy-start(bf16[1,128,1024]{2,1,0:T(8,128)(2,1)} %v_hbm.1) | copy-start | bytes 786436
  4.1 0.9 %copy-start.3 = (bf16[1,128,1024]{2,1,0:T(8,128)(2,1)S(1)}, bf16[1,128,1024]{2,1,0:T(8,128)(2,1)}, u32[]{:S(2)}) copy-start(bf16[1,128,1024]{2,1,0:T(8,128)(2,1)} %gate_hbm.1) | copy-start | bytes 786436
  5.1 0.9 %copy-start.4 = (bf16[1,128,1024]{2,1,0:T(8,128)(2,1)S(1)}, bf16[1,128,1024]{2,1,0:T(8,128)(2,1)}, u32[]{:S(2)}) copy-start(bf16[1,128,1024]{2,1,0:T(8,128)(2,1)} %grad_hbm.1) | copy-start | bytes 786436
  6.0 0.7 %copy-start.5 = (f32[1024]{0:T(1024)S(1)}, f32[1024]{0:T(1024)}, u32[]{:S(2)}) copy-start(f32[1024]{0:T(1024)} %param.12) | copy-start | bytes 12292

commit v2 on v1

--- a/solution.py
+++ b/solution.py
@@ -11,6 +11,8 @@
 H = 8
 MESH = pl.DeviceIdType.MESH
 K, V, Q, G = 0, 1, 2, 3
+PIECES = 2
+ROOM = 60 * 1024 * 1024
 
 
 def dot_nt(a, b):
@@ -29,12 +31,12 @@
 
 def kernel(
     n, m, reach, scale,
-    lens_ref, gain_ref, q_hbm, k_hbm, v_hbm, gate_hbm, grad_hbm,
-    out_hbm, gq_hbm, gk_hbm, gv_hbm, gg_hbm, ggain_ref,
-    blocks, gate, grad, row_probs, row_slope, col_probs, col_slope,
+    lens_hbm, gain_hbm, q_hbm, k_hbm, v_hbm, gate_hbm, grad_hbm,
+    out_hbm, gq_hbm, gk_hbm, gv_hbm, gg_hbm, ggain_hbm,
+    lens_ref, gain_ref, blocks, gate, grad, row_probs, row_slope, col_probs, col_slope,
     attended, gq_sum, gk_sum, gv_sum, results,
-    part, seq_parts, total, own_parts,
-    load_sem, store_sem, send_sem, recv_sem, seq_send, seq_recv, own_send, own_recv,
+    part, seq_parts, total, own_parts, part_sum,
+    load_sem, store_sem, send_sem, recv_sem, relay_sem, seq_send, seq_recv, own_send, own_recv,
 ):
     me = lax.axis_index("seq")
     mine = lax.axis_index("own")
@@ -42,6 +44,8 @@
     head = width // H
     users = lens_ref.shape[1]
     hbm = {K: k_hbm, V: v_hbm, Q: q_hbm}
+    relayed = n == 4 and reach == 2
+    piece = rows // PIECES
 
     def cols(h):
         return slice(h * head, (h + 1) * head)
@@ -62,6 +66,8 @@
         load(2, v_hbm.at[0], blocks.at[V, 0]),
         load(3, gate_hbm.at[0], gate),
         load(4, grad_hbm.at[0], grad),
+        load(5, gain_hbm, gain_ref),
+        load(6, lens_hbm, lens_ref),
     ]
     for copy in loads:
         copy.start()
@@ -78,35 +84,72 @@
 
     pl.semaphore_wait(barrier, n + m - 2)
 
-    def send(what, d):
-        peer = me + d if what in (K, V) else me - d
-        src = blocks.at[G, 0] if what == G else hbm[what].at[0]
+    def later(what):
+        return what in (K, V)
+
+    def span(c):
+        return pl.ds(c * piece, piece)
+
+    def send(what, d, c):
+        src = blocks.at[G, 0, span(c)] if what == G else hbm[what].at[0, span(c)]
         return pltpu.make_async_remote_copy(
-            src_ref=src, dst_ref=blocks.at[what, d],
-            send_sem=send_sem.at[what, d], recv_sem=recv_sem.at[what, d],
-            device_id={"seq": peer}, device_id_type=MESH,
+            src_ref=src, dst_ref=blocks.at[what, d, span(c)],
+            send_sem=send_sem.at[what, d, c], recv_sem=recv_sem.at[what, d, c],
+            device_id={"seq": me + d if later(what) else me - d}, device_id_type=MESH,
         )
 
+    def relay(what, c):
+        return pltpu.make_async_remote_copy(
+            src_ref=blocks.at[what, 2, span(c)], dst_ref=blocks.at[what, 1, span(c)],
+            send_sem=relay_sem.at[what, c], recv_sem=recv_sem.at[what, 1, c],
+            device_id={"seq": 2 if later(what) else 1}, device_id_type=MESH,
+        )
+
     def can_send(what, d):
-        return me + d < n if what in (K, V) else me >= d
-
-    def start(what):
+        ok = me + d < n if later(what) else me >= d
+        if relayed and d == 1:
+            ok = ok & (me != (1 if later(what) else 2))
+        return ok
+
+    def start(what, pieces):
         def body(d):
             @pl.when(can_send(what, d))
             def _():
-                send(what, d).start()
+                for c in pieces:
+                    send(what, d, c).start()
         steps(1, body)
 
     def wait_sends(what):
         def body(d):
             @pl.when(can_send(what, d))
             def _():
-                send(what, d).wait_send()
+                for c in range(PIECES):
+                    send(what, d, c).wait_send()
         steps(1, body)
 
-    start(K)
-    start(V)
-    start(Q)
+    def arrive(what, d):
+        for c in range(PIECES):
+            send(what, d, c).wait_recv()
+
+    def arrive_and_relay(what):
+        for c in range(PIECES):
+            send(what, 2, c).wait_recv()
+            relay(what, c).start()
+
+    everything = range(PIECES)
+    start(K, everything)
+    start(V, everything)
+    if relayed:
+        @pl.when(me != 3)
+        def _():
+            start(Q, everything)
+
+        @pl.when(me == 3)
+        def _():
+            for c in everything:
+                send(Q, 2, c).start()
+    else:
+        start(Q, everything)
 
     def weight(row_block, col_block, row_dim):
         t = row_block * rows + lax.broadcasted_iota(jnp.int32, (rows, rows), row_dim)
@@ -122,14 +165,12 @@
         inverse = 1.0 / span.astype(jnp.float32)
         return jnp.where((s >= first) & (s <= t), inverse, 0.0)
 
-    for copy in loads[:3]:
+    for copy in loads[:3] + loads[5:]:
         copy.wait()
 
     def row_scores(d):
         @pl.when(me >= d)
         def _():
-            if not isinstance(d, int) or d > 0:
-                send(K, d).wait_recv()
             w = weight(me, me - d, 0)
             for h in range(H):
                 scores = dot_nt(blocks[Q, 0, :, cols(h)], blocks[K, d, :, cols(h)]) * scale
@@ -140,42 +181,73 @@
     def row_attend(d):
         @pl.when(me >= d)
         def _():
-            send(V, d).wait_recv()
             for h in range(H):
                 attended[:, cols(h)] += dot_nn(row_probs[d, h], blocks[V, d, :, cols(h)])
+
+    def row_arrive(what):
+        if relayed:
+            @pl.when(me == 3)
+            def _():
+                arrive_and_relay(what)
+                arrive(what, 1)
+
+            @pl.when((me > 0) & (me < 3))
+            def _():
+                arrive(what, 1)
+
+            @pl.when(me == 2)
+            def _():
+                arrive(what, 2)
+        else:
+            def body(d):
+                @pl.when(me >= d)
+                def _():
+                    arrive(what, d)
+            steps(1, body)
 
     row_scores(0)
     for h in range(H):
         attended[:, cols(h)] = dot_nn(row_probs[0, h], blocks[V, 0, :, cols(h)])
+    row_arrive(K)
     steps(1, row_scores)
+    row_arrive(V)
+    if relayed:
+        @pl.when(me == 3)
+        def _():
+            for c in everything:
+                send(Q, 1, c).start()
     steps(1, row_attend)
 
-    for copy in loads[3:]:
+    for copy in loads[3:5]:
         copy.wait()
     gain = gain_ref[...]
-    step = 32 if rows % 32 == 0 else rows
+    step = 32 if piece % 32 == 0 else piece
+    for c in everything:
+        for r in range(c * piece, (c + 1) * piece, step):
+            at = slice(r, r + step)
+            att = attended[at, :]
+            center = att - jnp.mean(att, axis=1, keepdims=True)
+            rstd = lax.rsqrt(jnp.mean(center * center, axis=1, keepdims=True) + 1e-05)
+            normed = center * rstd
+            dnorm = grad[at, :].astype(jnp.float32) * gate[at, :].astype(jnp.float32) * gain
+            back = rstd * (
+                dnorm
+                - jnp.mean(dnorm, axis=1, keepdims=True)
+                - normed * jnp.mean(dnorm * normed, axis=1, keepdims=True)
+            )
+            attended[at, :] = normed
+            blocks[G, 0, at, :] = back.astype(jnp.bfloat16)
+        start(G, [c])
+
     share = jnp.zeros((1, width), jnp.float32)
     for r in range(0, rows, step):
         at = slice(r, r + step)
-        att = attended[at, :]
-        center = att - jnp.mean(att, axis=1, keepdims=True)
-        rstd = lax.rsqrt(jnp.mean(center * center, axis=1, keepdims=True) + 1e-05)
-        normed = center * rstd
+        normed = attended[at, :]
         gate_f = gate[at, :].astype(jnp.float32)
         grad_f = grad[at, :].astype(jnp.float32)
-        scaled = normed * gain
-        results[0, at, :] = (scaled * gate_f).astype(jnp.bfloat16)
-        results[1, at, :] = (grad_f * scaled).astype(jnp.bfloat16)
-        both = grad_f * gate_f
-        share = share + jnp.sum(both * normed, axis=0, keepdims=True)
-        dnorm = both * gain
-        back = rstd * (
-            dnorm
-            - jnp.mean(dnorm, axis=1, keepdims=True)
-            - normed * jnp.mean(dnorm * normed, axis=1, keepdims=True)
-        )
-        blocks[G, 0, at, :] = back.astype(jnp.bfloat16)
-    start(G)
+        results[0, at, :] = (normed * gain * gate_f).astype(jnp.bfloat16)
+        results[1, at, :] = (grad_f * normed * gain).astype(jnp.bfloat16)
+        share = share + jnp.sum(grad_f * gate_f * normed, axis=0, keepdims=True)
     part[...] = share
 
     def seq_share(j):
@@ -197,6 +269,11 @@
 
     def store(i, dst):
         return pltpu.make_async_copy(results.at[i], dst.at[0], store_sem.at[i])
+
+    if relayed:
+        @pl.when(me == 0)
+        def _():
+            arrive_and_relay(Q)
 
     stores = [store(i, dst) for i, dst in enumerate((out_hbm, gg_hbm, gq_hbm, gk_hbm, gv_hbm))]
     stores[0].start()
@@ -238,8 +315,12 @@
     def col_scores(d):
         @pl.when(me + d < n)
         def _():
-            if not isinstance(d, int) or d > 0:
-                send(Q, d).wait_recv()
+            if not isinstance(d, int):
+                arrive(Q, d)
+            elif d == 2 and relayed:
+                pl.when(me != 0)(lambda: arrive(Q, d))
+            elif d > 0:
+                arrive(Q, d)
             w = weight(me + d, me, 1)
             for h in range(H):
                 scores = dot_nt(blocks[K, 0, :, cols(h)], blocks[Q, d, :, cols(h)]) * scale
@@ -251,8 +332,8 @@
         @pl.when(me + d < n)
         def _():
             own = isinstance(d, int) and d == 0
-            if not own:
-                send(G, d).wait_recv()
+            if not own and not (relayed and d == 2):
+                arrive(G, d)
             for h in range(H):
                 back = blocks[G, d, :, cols(h)]
                 grad_probs = dot_nt(blocks[V, 0, :, cols(h)], back)
@@ -269,7 +350,19 @@
     col_scores(0)
     steps(1, col_scores)
     col_back(0)
-    steps(1, col_back)
+    if relayed:
+        @pl.when(me == 0)
+        def _():
+            arrive_and_relay(G)
+
+        @pl.when(me == 1)
+        def _():
+            arrive(G, 2)
+
+        col_back(2)
+        col_back(1)
+    else:
+        steps(1, col_back)
     results[3] = (gk_sum[...] * scale).astype(jnp.bfloat16)
     results[4] = gv_sum[...].astype(jnp.bfloat16)
     stores[3].start()
@@ -287,13 +380,30 @@
     whole = own_parts[0]
     for j in range(1, m):
         whole = whole + own_parts[j]
-    ggain_ref[...] = whole
+    part_sum[...] = whole
+    last = pltpu.make_async_copy(part_sum, ggain_hbm, store_sem.at[5])
+    last.start()
 
     for what in (K, V, Q, G):
         wait_sends(what)
+    if relayed:
+        for what in (K, V, Q, G):
+            @pl.when(me == (3 if later(what) else 0))
+            def _():
+                for c in everything:
+                    relay(what, c).wait_send()
     pl.loop(1, n)(lambda j: seq_share(j).wait_send())
     pl.loop(1, m)(lambda j: own_share(j).wait_send())
-    for copy in stores:
+    for copy in stores + [last]:
+        copy.wait()
+
+
+def finish(*refs):
+    sources, results, sem = refs[:6], refs[6:12], refs[12]
+    copies = [pltpu.make_async_copy(a, b, sem.at[i]) for i, (a, b) in enumerate(zip(sources, results))]
+    for copy in copies:
+        copy.start()
+    for copy in copies:
         copy.wait()
 
 
@@ -302,16 +412,19 @@
     head = width // H
     reach = min(n - 1, (rows * n // 2 - 1) // rows + 1)
     slots = reach + 1
+    hbm = pl.BlockSpec(memory_space=pltpu.HBM)
     any_spec = pl.BlockSpec(memory_space=pl.ANY)
-    vmem = pl.BlockSpec(memory_space=pltpu.VMEM)
     block = jax.ShapeDtypeStruct(queries.shape, jnp.bfloat16)
+    shapes = [block] * 5 + [jax.ShapeDtypeStruct((1, width), jnp.float32)]
     dma = pltpu.SemaphoreType.DMA
     outs = pl.pallas_call(
         functools.partial(kernel, n, m, reach, 1.0 / math.sqrt(head)),
-        out_shape=[block] * 5 + [jax.ShapeDtypeStruct((1, width), jnp.float32)],
-        in_specs=[pl.BlockSpec(memory_space=pltpu.SMEM), vmem] + [any_spec] * 5,
-        out_specs=[any_spec] * 5 + [vmem],
+        out_shape=shapes,
+        in_specs=[hbm] * 7,
+        out_specs=[any_spec] * 6,
         scratch_shapes=[
+            pltpu.SMEM(lengths.shape, jnp.int32),
+            pltpu.VMEM((1, width), jnp.float32),
             pltpu.VMEM((4, slots, rows, width), jnp.bfloat16),
             pltpu.VMEM((rows, width), jnp.bfloat16),
             pltpu.VMEM((rows, width), jnp.bfloat16),
@@ -328,17 +441,25 @@
             pltpu.VMEM((n, 1, width), jnp.float32),
             pltpu.VMEM((1, width), jnp.float32),
             pltpu.VMEM((m, 1, width), jnp.float32),
-            dma((5,)), dma((5,)), dma((4, slots)), dma((4, slots)),
+            pltpu.VMEM((1, width), jnp.float32),
+            dma((7,)), dma((6,)), dma((4, slots, PIECES)), dma((4, slots, PIECES)), dma((4, PIECES)),
             dma((n,)), dma((n,)), dma((m,)), dma((m,)),
         ],
         compiler_params=pltpu.CompilerParams(
-            collective_id=0, has_side_effects=True, vmem_limit_bytes=44 * 1024 * 1024
+            collective_id=0, has_side_effects=True, vmem_limit_bytes=ROOM
         ),
         cost_estimate=pl.CostEstimate(
             flops=16 * slots * rows * rows * width, bytes_accessed=20 * rows * width, transcendentals=0
         ),
     )(lengths, gain.reshape(1, width), queries, keys, values, gates, grad_out)
-    output, grad_q, grad_k, grad_v, grad_gate, grad_gain = outs
+    output, grad_q, grad_k, grad_v, grad_gate, grad_gain = pl.pallas_call(
+        finish,
+        out_shape=shapes,
+        in_specs=[any_spec] * 6,
+        out_specs=[any_spec] * 6,
+        scratch_shapes=[dma((6,))],
+        compiler_params=pltpu.CompilerParams(has_side_effects=True, vmem_limit_bytes=ROOM),
+    )(*outs)
     return output, grad_q, grad_k, grad_v, grad_gate, grad_gain.reshape(width)
 
 

time: 53.8 us -> 85.5 us (1.59)
  the two profiles are of different devices: /device:TPU:0 before, /device:TPU:2 now
where the time goes in v2:
time: 85.5 us; the launch traced here: 85.4 us
  Pallas kernels  84.7 us (99%)
    pallas_call x1, Pallas kernels, per_device(): pl.pallas_call(functools.partial(kernel, n, m, reach, 1.0 / math.sqrt(hea...  43.7 us
    pallas_call x1, Pallas kernels, per_device(): pl.pallas_call(finish, out_shape=shapes, in_specs=[any_spec] * 6, out_spe...  41 us

profile of v2, /device:TPU:2, one launch (start us, length us, event | category | flops | bytes accessed | tf_op | source)
XLA Modules:
  0.0 85.4 jit_solution(9003899291510852038)
XLA Ops:
  0.6 43.7 %shard_map.118 = (bf16[1,128,1024]{2,1,0:T(8,128)(2,1)}, bf16[1,128,1024]{2,1,0:T(8,128)(2,1)}, bf16[1,128,1024]{2,1,0:T(8,128)(2,1)}, bf16[1,128,1024]{2,1,0:T(...) custom-call(s32[1,4]{1,0:T(1,128)} %lens_hbm.1, f32[1,1024]{1,0:T(1,128)} %bitcast.2, ...), custom_call_target="tpu_custom_call" | custom-call | flops 805306368 | bytes 2621440 | tf_op jit(solution)/shard_map/pallas_call | solution.py:420
  44.4 41.0 %shard_map.119 = (bf16[1,128,1024]{2,1,0:T(8,128)(2,1)}, bf16[1,128,1024]{2,1,0:T(8,128)(2,1)}, bf16[1,128,1024]{2,1,0:T(8,128)(2,1)}, bf16[1,128,1024]{2,1,0:T(...) custom-call(bf16[1,128,1024]{2,1,0:T(8,128)(2,1)} %get-tuple-element.18.refs_0_, ...), custom_call_target="tpu_custom_call" | custom-call | tf_op jit(solution)/shard_map/pallas_call | solution.py:455

commit v3 on v2

v3 whole, which is shorter than its diff:
```python
import functools
import math

import jax
import jax.numpy as jnp
from jax import lax
from jax.experimental import pallas as pl
from jax.experimental.pallas import tpu as pltpu
from jax.sharding import PartitionSpec as P

H = 8
MESH = pl.DeviceIdType.MESH
K, V, Q, G = 0, 1, 2, 3
PIECES = 2
ROOM = 60 * 1024 * 1024


def dot_nt(a, b):
    return lax.dot_general(a, b, (((1,), (1,)), ((), ())), preferred_element_type=jnp.float32)


def dot_nn(a, b):
    return lax.dot_general(a, b, (((1,), (0,)), ((), ())), preferred_element_type=jnp.float32)


def silu_and_slope(scores):
    sig = 0.5 * jnp.tanh(0.5 * scores) + 0.5
    silu = scores * sig
    return silu, sig + silu * (1.0 - sig)


def kernel(
    n, m, reach, wide, scale,
    lens_hbm, gain_hbm, q_hbm, k_hbm, v_hbm, gate_hbm, grad_hbm,
    out_hbm, gq_hbm, gk_hbm, gv_hbm, gg_hbm, ggain_hbm,
    lens_ref, gain_ref, blocks, gate, grad,
    row_probs, row_slope, col_probs, col_slope,
    far_row_probs, far_row_slope, far_col_probs, far_col_slope,
    attended, gq_sum, gk_sum, gv_sum, results,
    part, seq_parts, total, own_parts, part_sum,
    load_sem, store_sem, send_sem, recv_sem, relay_sem, seq_send, seq_recv, own_send, own_recv,
):
    me = lax.axis_index("seq")
    mine = lax.axis_index("own")
    rows, width = gate.shape
    head = width // H
    users = lens_ref.shape[1]
    groups = reach // wide
    relayed = n == 4 and reach == 2
    piece = rows // PIECES
    everything = range(PIECES)

    def near(what, h):
        return blocks[what, 0, :, h]

    def far(what, first, h):
        return blocks[what, pl.ds(first, wide), :, h].reshape(wide * rows, head)

    def each_head(count, body):
        @pl.loop(0, H // count)
        def _(i):
            for j in range(count):
                h = i * count + j
                body(h, pl.ds(pl.multiple_of(h * head, head), head))

    def load(i, src, dst):
        return pltpu.make_async_copy(src, dst, load_sem.at[i])

    loads = [
        load(0, k_hbm.at[0], blocks.at[K, 0]),
        load(1, v_hbm.at[0], blocks.at[V, 0]),
        load(2, q_hbm.at[0], blocks.at[Q, 0]),
        load(3, gate_hbm.at[0], gate),
        load(4, grad_hbm.at[0], grad),
        load(5, gain_hbm, gain_ref),
        load(6, lens_hbm, lens_ref),
    ]
    for copy in loads:
        copy.start()

    barrier = pltpu.get_barrier_semaphore()

    @pl.loop(1, n)
    def _(j):
        pl.semaphore_signal(barrier, 1, device_id={"seq": lax.rem(me + j, n)}, device_id_type=MESH)

    @pl.loop(1, m)
    def _(j):
        pl.semaphore_signal(barrier, 1, device_id={"own": lax.rem(mine + j, m)}, device_id_type=MESH)

    for copy in loads[:3]:
        copy.wait()
    pl.semaphore_wait(barrier, n + m - 2)

    def later(what):
        return what in (K, V)

    def span(c):
        return pl.ds(c * piece, piece)

    def send(what, d, c):
        return pltpu.make_async_remote_copy(
            src_ref=blocks.at[what, 0, span(c)], dst_ref=blocks.at[what, d, span(c)],
            send_sem=send_sem.at[what, d, c], recv_sem=recv_sem.at[what, d, c],
            device_id={"seq": me + d if later(what) else me - d}, device_id_type=MESH,
        )

    def relay(what, c):
        return pltpu.make_async_remote_copy(
            src_ref=blocks.at[what, 2, span(c)], dst_ref=blocks.at[what, 1, span(c)],
            send_sem=relay_sem.at[what, c], recv_sem=recv_sem.at[what, 1, c],
            device_id={"seq": 2 if later(what) else 1}, device_id_type=MESH,
        )

    def can_send(what, d):
        ok = me + d < n if later(what) else me >= d
        if relayed and d == 1:
            ok = ok & (me != (1 if later(what) else 2))
        return ok

    def start(what, pieces):
        for d in range(1, reach + 1):
            @pl.when(can_send(what, d))
            def _():
                for c in pieces:
                    send(what, d, c).start()

    def wait_sends(what):
        for d in range(1, reach + 1):
            @pl.when(can_send(what, d))
            def _():
                for c in everything:
                    send(what, d, c).wait_send()

    def arrive(what, d):
        for c in everything:
            send(what, d, c).wait_recv()

    def arrive_and_relay(what):
        for c in everything:
            send(what, 2, c).wait_recv()
            relay(what, c).start()

    def arrive_group(what, first):
        for d in range(first, first + wide):
            pl.when(me >= d if later(what) else me + d < n)(functools.partial(arrive, what, d))

    def arrive_all(what):
        if relayed:
            relayer = 3 if later(what) else 0

            @pl.when(me == relayer)
            def _():
                arrive_and_relay(what)
                arrive(what, 1)

            pl.when(me != relayer)(functools.partial(arrive_group, what, 1))

    start(K, everything)
    start(V, everything)
    if relayed:
        pl.when(me != 3)(functools.partial(start, Q, everything))

        @pl.when(me == 3)
        def _():
            for c in everything:
                send(Q, 2, c).start()
    else:
        start(Q, everything)

    if wide == 2:
        for d in range(2, reach + 1, 2):
            @pl.when(me == d - 1)
            def _():
                blocks[K, d] = jnp.zeros((rows, width), jnp.bfloat16)
                blocks[V, d] = jnp.zeros((rows, width), jnp.bfloat16)

            @pl.when(me + d == n)
            def _():
                blocks[Q, d] = jnp.zeros((rows, width), jnp.bfloat16)
                blocks[G, d] = jnp.zeros((rows, width), jnp.bfloat16)

    def weight(t, s):
        first = jnp.zeros_like(t)
        length = jnp.ones_like(t)
        end = jnp.int32(0)
        for u in range(users):
            begin, end = end, end + lens_ref[0, u]
            inside = (t >= begin) & (t < end)
            first = jnp.where(inside, begin, first)
            length = jnp.where(inside, lens_ref[0, u], length)
        return jnp.where((s >= first) & (s <= t), 1.0 / length.astype(jnp.float32), 0.0)

    def iotas(columns):
        return [lax.broadcasted_iota(jnp.int32, (rows, columns), i) for i in (0, 1)]

    for copy in loads[5:]:
        copy.wait()

    def pointwise(scores, w, probs_ref, slope_ref):
        scores = scores * scale
        silu, slope = silu_and_slope(scores)
        probs = (silu * w).astype(jnp.bfloat16)
        probs_ref[...] = probs
        slope_ref[...] = slope * w
        return probs

    down, across = iotas(rows)
    w = weight(me * rows + down, me * rows + across)

    def near_forward(h, at):
        probs = pointwise(dot_nt(near(Q, at), near(K, at)), w, row_probs.at[h], row_slope.at[h])
        attended[:, at] = dot_nn(probs, near(V, at))

    each_head(2, near_forward)

    arrive_all(K)
    for g in range(groups):
        first = 1 + g * wide

        @pl.when(me >= first)
        def _():
            if not relayed:
                arrive_group(K, first)
            down, across = iotas(wide * rows)
            s = (me - first) * rows + across - jnp.where(across >= rows, 2 * rows, 0)
            w = weight(me * rows + down, s)

            def body(h, at):
                scores = dot_nt(near(Q, at), far(K, first, at))
                pointwise(scores, w, far_row_probs.at[g, h], far_row_slope.at[g, h])

            each_head(1, body)

    arrive_all(V)
    if relayed:
        @pl.when(me == 3)
        def _():
            for c in everything:
                send(Q, 1, c).start()
    for g in range(groups):
        first = 1 + g * wide

        @pl.when(me >= first)
        def _():
            if not relayed:
                arrive_group(V, first)

            def body(h, at):
                attended[:, at] += dot_nn(far_row_probs[g, h], far(V, first, at))

            each_head(2, body)

    for copy in loads[3:5]:
        copy.wait()
    gain = gain_ref[...]
    step = 32 if piece % 32 == 0 else piece

    @pl.loop(0, PIECES)
    def _(c):
        for r in range(0, piece, step):
            at = pl.ds(pl.multiple_of(c * piece + r, step), step)
            att = attended[at, :]
            center = att - jnp.mean(att, axis=1, keepdims=True)
            rstd = lax.rsqrt(jnp.mean(center * center, axis=1, keepdims=True) + 1e-05)
            normed = center * rstd
            dnorm = grad[at, :].astype(jnp.float32) * gate[at, :].astype(jnp.float32) * gain
            back = rstd * (
                dnorm
                - jnp.mean(dnorm, axis=1, keepdims=True)
                - normed * jnp.mean(dnorm * normed, axis=1, keepdims=True)
            )
            attended[at, :] = normed
            blocks[G, 0, at, :] = back.astype(jnp.bfloat16)
        start(G, [c])

    part[...] = jnp.zeros((1, width), jnp.float32)

    @pl.loop(0, rows // step)
    def _(i):
        at = pl.ds(pl.multiple_of(i * step, step), step)
        normed = attended[at, :]
        gate_f = gate[at, :].astype(jnp.float32)
        grad_f = grad[at, :].astype(jnp.float32)
        results[0, at, :] = (normed * gain * gate_f).astype(jnp.bfloat16)
        results[1, at, :] = (grad_f * normed * gain).astype(jnp.bfloat16)
        part[...] += jnp.sum(grad_f * gate_f * normed, axis=0, keepdims=True)

    def seq_share(j):
        return pltpu.make_async_remote_copy(
            src_ref=part, dst_ref=seq_parts.at[me],
            send_sem=seq_send.at[j], recv_sem=seq_recv.at[me],
            device_id={"seq": lax.rem(me + j, n)}, device_id_type=MESH,
        )

    def own_share(j):
        return pltpu.make_async_remote_copy(
            src_ref=total, dst_ref=own_parts.at[mine],
            send_sem=own_send.at[j], recv_sem=own_recv.at[mine],
            device_id={"own": lax.rem(mine + j, m)}, device_id_type=MESH,
        )

    pl.loop(1, n)(lambda j: seq_share(j).start())
    seq_parts[me] = part[...]

    def store(i, dst):
        return pltpu.make_async_copy(results.at[i], dst.at[0], store_sem.at[i])

    stores = [store(i, dst) for i, dst in enumerate((out_hbm, gg_hbm, gq_hbm, gk_hbm, gv_hbm))]
    stores[0].start()
    stores[1].start()

    arrive_all(Q)

    down, across = iotas(rows)
    near_w = weight(me * rows + across, me * rows + down)

    def near_column(h, at):
        pointwise(dot_nt(near(K, at), near(Q, at)), near_w, col_probs.at[h], col_slope.at[h])

    each_head(2, near_column)
    for g in range(groups):
        first = 1 + g * wide

        @pl.when(me + first < n)
        def _():
            if not relayed:
                arrive_group(Q, first)
            down, across = iotas(wide * rows)
            w = weight((me + first) * rows + across, me * rows + down)

            def body(h, at):
                scores = dot_nt(near(K, at), far(Q, first, at))
                pointwise(scores, w, far_col_probs.at[g, h], far_col_slope.at[g, h])

            each_head(1, body)

    def near_back(h, at):
        grad_probs = dot_nt(near(G, at), near(V, at))
        gq_sum[:, at] = dot_nn((grad_probs * row_slope[h]).astype(jnp.bfloat16), near(K, at))
        grad_probs = dot_nt(near(V, at), near(G, at))
        gk_sum[:, at] = dot_nn((grad_probs * col_slope[h]).astype(jnp.bfloat16), near(Q, at))
        gv_sum[:, at] = dot_nn(col_probs[h], near(G, at))

    each_head(2, near_back)
    for g in range(groups):
        first = 1 + g * wide

        @pl.when(me >= first)
        def _():
            def body(h, at):
                grad_probs = dot_nt(near(G, at), far(V, first, at))
                grad_scores = (grad_probs * far_row_slope[g, h]).astype(jnp.bfloat16)
                gq_sum[:, at] += dot_nn(grad_scores, far(K, first, at))

            each_head(1, body)

    results[2] = (gq_sum[...] * scale).astype(jnp.bfloat16)
    stores[2].start()

    arrive_all(G)
    @pl.loop(1, n)
    def _(j):
        src = lax.rem(me + j, n)
        pltpu.make_async_remote_copy(
            src_ref=part, dst_ref=seq_parts.at[src],
            send_sem=seq_send.at[j], recv_sem=seq_recv.at[src],
            device_id={"seq": src}, device_id_type=MESH,
        ).wait_recv()

    group = seq_parts[0]
    for j in range(1, n):
        group = group + seq_parts[j]
    total[...] = group
    pl.loop(1, m)(lambda j: own_share(j).start())
    own_parts[mine] = group

    for g in range(groups):
        first = 1 + g * wide

        @pl.when(me + first < n)
        def _():
            if not relayed:
                arrive_group(G, first)

            def body(h, at):
                back = far(G, first, at)
                grad_probs = dot_nt(near(V, at), back)
                grad_scores = (grad_probs * far_col_slope[g, h]).astype(jnp.bfloat16)
                gk_sum[:, at] += dot_nn(grad_scores, far(Q, first, at))
                gv_sum[:, at] += dot_nn(far_col_probs[g, h], back)

            each_head(1, body)

    results[3] = (gk_sum[...] * scale).astype(jnp.bfloat16)
    results[4] = gv_sum[...].astype(jnp.bfloat16)
    stores[3].start()
    stores[4].start()

    @pl.loop(1, m)
    def _(j):
        src = lax.rem(mine + j, m)
        pltpu.make_async_remote_copy(
            src_ref=total, dst_ref=own_parts.at[src],
            send_sem=own_send.at[j], recv_sem=own_recv.at[src],
            device_id={"own": src}, device_id_type=MESH,
        ).wait_recv()

    whole = own_parts[0]
    for j in range(1, m):
        whole = whole + own_parts[j]
    part_sum[...] = whole
    last = pltpu.make_async_copy(part_sum, ggain_hbm, store_sem.at[5])
    last.start()

    for what in (K, V, Q, G):
        wait_sends(what)
        if relayed:
            @pl.when(me == (3 if later(what) else 0))
            def _():
                for c in everything:
                    relay(what, c).wait_send()
    pl.loop(1, n)(lambda j: seq_share(j).wait_send())
    pl.loop(1, m)(lambda j: own_share(j).wait_send())
    for copy in stores + [last]:
        copy.wait()


def finish(*refs):
    sources, results, held, sem = refs[:6], refs[6:12], refs[12:18], refs[18]
    loads = [pltpu.make_async_copy(a, b, sem.at[0, i]) for i, (a, b) in enumerate(zip(sources, held))]
    stores = [pltpu.make_async_copy(a, b, sem.at[1, i]) for i, (a, b) in enumerate(zip(held, results))]
    for copy in loads:
        copy.start()
    for load, store in zip(loads, stores):
        load.wait()
        store.start()
    for copy in stores:
        copy.wait()


def per_device(n, m, queries, keys, values, gates, lengths, gain, grad_out):
    rows, width = queries.shape[1], queries.shape[2]
    head = width // H
    reach = min(n - 1, (rows * n // 2 - 1) // rows + 1)
    slots = reach + 1
    wide = 2 if reach % 2 == 0 else 1
    groups = reach // wide
    hbm = pl.BlockSpec(memory_space=pltpu.HBM)
    any_spec = pl.BlockSpec(memory_space=pl.ANY)
    block = jax.ShapeDtypeStruct(queries.shape, jnp.bfloat16)
    shapes = [block] * 5 + [jax.ShapeDtypeStruct((1, width), jnp.float32)]
    dma = pltpu.SemaphoreType.DMA
    outs = pl.pallas_call(
        functools.partial(kernel, n, m, reach, wide, 1.0 / math.sqrt(head)),
        out_shape=shapes,
        in_specs=[hbm] * 7,
        out_specs=[any_spec] * 6,
        scratch_shapes=[
            pltpu.SMEM(lengths.shape, jnp.int32),
            pltpu.VMEM((1, width), jnp.float32),
            pltpu.VMEM((4, slots, rows, width), jnp.bfloat16),
            pltpu.VMEM((rows, width), jnp.bfloat16),
            pltpu.VMEM((rows, width), jnp.bfloat16),
            pltpu.VMEM((H, rows, rows), jnp.bfloat16),
            pltpu.VMEM((H, rows, rows), jnp.float32),
            pltpu.VMEM((H, rows, rows), jnp.bfloat16),
            pltpu.VMEM((H, rows, rows), jnp.float32),
            pltpu.VMEM((groups, H, rows, wide * rows), jnp.bfloat16),
            pltpu.VMEM((groups, H, rows, wide * rows), jnp.float32),
            pltpu.VMEM((groups, H, rows, wide * rows), jnp.bfloat16),
            pltpu.VMEM((groups, H, rows, wide * rows), jnp.float32),
            pltpu.VMEM((rows, width), jnp.float32),
            pltpu.VMEM((rows, width), jnp.float32),
            pltpu.VMEM((rows, width), jnp.float32),
            pltpu.VMEM((rows, width), jnp.float32),
            pltpu.VMEM((5, rows, width), jnp.bfloat16),
            pltpu.VMEM((1, width), jnp.float32),
            pltpu.VMEM((n, 1, width), jnp.float32),
            pltpu.VMEM((1, width), jnp.float32),
            pltpu.VMEM((m, 1, width), jnp.float32),
            pltpu.VMEM((1, width), jnp.float32),
            dma((7,)), dma((6,)), dma((4, slots, PIECES)), dma((4, slots, PIECES)), dma((4, PIECES)),
            dma((n,)), dma((n,)), dma((m,)), dma((m,)),
        ],
        compiler_params=pltpu.CompilerParams(
            collective_id=0, has_side_effects=True, vmem_limit_bytes=ROOM
        ),
        cost_estimate=pl.CostEstimate(
            flops=16 * slots * rows * rows * width, bytes_accessed=20 * rows * width, transcendentals=0
        ),
    )(lengths, gain.reshape(1, width), queries, keys, values, gates, grad_out)
    output, grad_q, grad_k, grad_v, grad_gate, grad_gain = pl.pallas_call(
        finish,
        out_shape=shapes,
        in_specs=[any_spec] * 6,
        out_specs=[any_spec] * 6,
        scratch_shapes=[pltpu.VMEM(x.shape, x.dtype) for x in shapes] + [dma((2, 6))],
        compiler_params=pltpu.CompilerParams(has_side_effects=True, vmem_limit_bytes=ROOM),
    )(*outs)
    return output, grad_q, grad_k, grad_v, grad_gate, grad_gain.reshape(width)


def solution(mesh):
    blocked = P("own", "seq", None)
    sizes = (mesh.shape["seq"], mesh.shape["own"])
    return jax.shard_map(
        functools.partial(per_device, *sizes),
        mesh=mesh,
        in_specs=(blocked, blocked, blocked, blocked, P("own", None), P(), blocked),
        out_specs=(blocked, blocked, blocked, blocked, blocked, P()),
        check_vma=False,
    )
```

time: 85.5 us -> 43.9 us (0.51)
  the two profiles are of different devices: /device:TPU:2 before, /device:TPU:5 now
where the time goes in v3:
time: 43.9 us; the launch traced here: 43.7 us
  Pallas kernels  43.1 us (98%)
  between operations  0.64 us (1%)
    pallas_call x1, Pallas kernels, per_device(): pl.pallas_call(functools.partial(kernel, n, m, reach, wide, 1.0 / math.sq...  41 us
    pallas_call x1, Pallas kernels, per_device(): pl.pallas_call(finish, out_shape=shapes, in_specs=[any_spec] * 6, out_spe...  2.11 us

profile of v3, /device:TPU:5, one launch (start us, length us, event | category | flops | bytes accessed | tf_op | source)
XLA Modules:
  0.0 43.7 jit_solution(16091502763128247283)
XLA Ops:
  0.6 41.0 %shard_map.118 = (bf16[1,128,1024]{2,1,0:T(8,128)(2,1)}, bf16[1,128,1024]{2,1,0:T(8,128)(2,1)}, bf16[1,128,1024]{2,1,0:T(8,128)(2,1)}, bf16[1,128,1024]{2,1,0:T(...) custom-call(s32[1,4]{1,0:T(1,128)} %lens_hbm.1, f32[1,1024]{1,0:T(1,128)} %bitcast.2, ...), custom_call_target="tpu_custom_call" | custom-call | flops 805306368 | bytes 2621440 | tf_op jit(solution)/shard_map/pallas_call | solution.py:454
  41.6 2.1 %shard_map.119 = (bf16[1,128,1024]{2,1,0:T(8,128)(2,1)}, bf16[1,128,1024]{2,1,0:T(8,128)(2,1)}, bf16[1,128,1024]{2,1,0:T(8,128)(2,1)}, bf16[1,128,1024]{2,1,0:T(...) custom-call(bf16[1,128,1024]{2,1,0:T(8,128)(2,1)} %get-tuple-element.18.refs_0_, ...), custom_call_target="tpu_custom_call" | custom-call | tf_op jit(solution)/shard_map/pallas_call | solution.py:493

commit v4 on v3

--- a/solution.py
+++ b/solution.py
@@ -11,7 +11,8 @@
 H = 8
 MESH = pl.DeviceIdType.MESH
 K, V, Q, G = 0, 1, 2, 3
-PIECES = 2
+PIECES = 4
+HALVES = 2
 ROOM = 60 * 1024 * 1024
 
 
@@ -56,6 +57,10 @@
     def far(what, first, h):
         return blocks[what, pl.ds(first, wide), :, h].reshape(wide * rows, head)
 
+    def far_half(what, first, wide, half, h):
+        length = rows // HALVES
+        return blocks[what, pl.ds(first, wide), pl.ds(half * length, length), h].reshape(wide * length, head)
+
     def each_head(count, body):
         @pl.loop(0, H // count)
         def _(i):
@@ -96,7 +101,7 @@
         return what in (K, V)
 
     def span(c):
-        return pl.ds(c * piece, piece)
+        return pl.ds(c * piece if isinstance(c, int) else pl.multiple_of(c * piece, piece), piece)
 
     def send(what, d, c):
         return pltpu.make_async_remote_copy(
@@ -132,29 +137,29 @@
                 for c in everything:
                     send(what, d, c).wait_send()
 
-    def arrive(what, d):
-        for c in everything:
+    def arrive(what, d, pieces=everything):
+        for c in pieces:
             send(what, d, c).wait_recv()
 
-    def arrive_and_relay(what):
-        for c in everything:
+    def arrive_and_relay(what, pieces=everything):
+        for c in pieces:
             send(what, 2, c).wait_recv()
             relay(what, c).start()
 
-    def arrive_group(what, first):
+    def arrive_group(what, first, pieces=everything):
         for d in range(first, first + wide):
-            pl.when(me >= d if later(what) else me + d < n)(functools.partial(arrive, what, d))
-
-    def arrive_all(what):
+            pl.when(me >= d if later(what) else me + d < n)(functools.partial(arrive, what, d, pieces))
+
+    def arrive_all(what, pieces=everything):
         if relayed:
             relayer = 3 if later(what) else 0
 
             @pl.when(me == relayer)
             def _():
-                arrive_and_relay(what)
-                arrive(what, 1)
-
-            pl.when(me != relayer)(functools.partial(arrive_group, what, 1))
+                arrive_and_relay(what, pieces)
+                arrive(what, 1, pieces)
+
+            pl.when(me != relayer)(functools.partial(arrive_group, what, 1, pieces))
 
     start(K, everything)
     start(V, everything)
@@ -165,6 +170,8 @@
         def _():
             for c in everything:
                 send(Q, 2, c).start()
+            for c in everything[: PIECES // 2]:
+                send(Q, 1, c).start()
     else:
         start(Q, everything)
 
@@ -174,11 +181,6 @@
             def _():
                 blocks[K, d] = jnp.zeros((rows, width), jnp.bfloat16)
                 blocks[V, d] = jnp.zeros((rows, width), jnp.bfloat16)
-
-            @pl.when(me + d == n)
-            def _():
-                blocks[Q, d] = jnp.zeros((rows, width), jnp.bfloat16)
-                blocks[G, d] = jnp.zeros((rows, width), jnp.bfloat16)
 
     def weight(t, s):
         first = jnp.zeros_like(t)
@@ -212,7 +214,14 @@
         probs = pointwise(dot_nt(near(Q, at), near(K, at)), w, row_probs.at[h], row_slope.at[h])
         attended[:, at] = dot_nn(probs, near(V, at))
 
-    each_head(2, near_forward)
+    each_head(4, near_forward)
+
+    near_w = weight(me * rows + across, me * rows + down)
+
+    def near_column(h, at):
+        pointwise(dot_nt(near(K, at), near(Q, at)), near_w, col_probs.at[h], col_slope.at[h])
+
+    each_head(4, near_column)
 
     arrive_all(K)
     for g in range(groups):
@@ -230,13 +239,13 @@
                 scores = dot_nt(near(Q, at), far(K, first, at))
                 pointwise(scores, w, far_row_probs.at[g, h], far_row_slope.at[g, h])
 
-            each_head(1, body)
+            each_head(4, body)
 
     arrive_all(V)
     if relayed:
         @pl.when(me == 3)
         def _():
-            for c in everything:
+            for c in everything[PIECES // 2 :]:
                 send(Q, 1, c).start()
     for g in range(groups):
         first = 1 + g * wide
@@ -249,17 +258,18 @@
             def body(h, at):
                 attended[:, at] += dot_nn(far_row_probs[g, h], far(V, first, at))
 
-            each_head(2, body)
+            each_head(4, body)
 
     for copy in loads[3:5]:
         copy.wait()
     gain = gain_ref[...]
-    step = 32 if piece % 32 == 0 else piece
-
-    @pl.loop(0, PIECES)
-    def _(c):
-        for r in range(0, piece, step):
-            at = pl.ds(pl.multiple_of(c * piece + r, step), step)
+    step = piece
+
+    @pl.loop(0, HALVES)
+    def _(half):
+        pieces = [half * (PIECES // HALVES) + c for c in range(PIECES // HALVES)]
+        for c in pieces:
+            at = span(c)
             att = attended[at, :]
             center = att - jnp.mean(att, axis=1, keepdims=True)
             rstd = lax.rsqrt(jnp.mean(center * center, axis=1, keepdims=True) + 1e-05)
@@ -272,7 +282,7 @@
             )
             attended[at, :] = normed
             blocks[G, 0, at, :] = back.astype(jnp.bfloat16)
-        start(G, [c])
+        start(G, pieces)
 
     part[...] = jnp.zeros((1, width), jnp.float32)
 
@@ -310,31 +320,6 @@
     stores[0].start()
     stores[1].start()
 
-    arrive_all(Q)
-
-    down, across = iotas(rows)
-    near_w = weight(me * rows + across, me * rows + down)
-
-    def near_column(h, at):
-        pointwise(dot_nt(near(K, at), near(Q, at)), near_w, col_probs.at[h], col_slope.at[h])
-
-    each_head(2, near_column)
-    for g in range(groups):
-        first = 1 + g * wide
-
-        @pl.when(me + first < n)
-        def _():
-            if not relayed:
-                arrive_group(Q, first)
-            down, across = iotas(wide * rows)
-            w = weight((me + first) * rows + across, me * rows + down)
-
-            def body(h, at):
-                scores = dot_nt(near(K, at), far(Q, first, at))
-                pointwise(scores, w, far_col_probs.at[g, h], far_col_slope.at[g, h])
-
-            each_head(1, body)
-
     def near_back(h, at):
         grad_probs = dot_nt(near(G, at), near(V, at))
         gq_sum[:, at] = dot_nn((grad_probs * row_slope[h]).astype(jnp.bfloat16), near(K, at))
@@ -342,7 +327,7 @@
         gk_sum[:, at] = dot_nn((grad_probs * col_slope[h]).astype(jnp.bfloat16), near(Q, at))
         gv_sum[:, at] = dot_nn(col_probs[h], near(G, at))
 
-    each_head(2, near_back)
+    each_head(4, near_back)
     for g in range(groups):
         first = 1 + g * wide
 
@@ -353,44 +338,80 @@
                 grad_scores = (grad_probs * far_row_slope[g, h]).astype(jnp.bfloat16)
                 gq_sum[:, at] += dot_nn(grad_scores, far(K, first, at))
 
-            each_head(1, body)
+            each_head(4, body)
 
     results[2] = (gq_sum[...] * scale).astype(jnp.bfloat16)
     stores[2].start()
 
-    arrive_all(G)
-    @pl.loop(1, n)
-    def _(j):
-        src = lax.rem(me + j, n)
-        pltpu.make_async_remote_copy(
-            src_ref=part, dst_ref=seq_parts.at[src],
-            send_sem=seq_send.at[j], recv_sem=seq_recv.at[src],
-            device_id={"seq": src}, device_id_type=MESH,
-        ).wait_recv()
-
-    group = seq_parts[0]
-    for j in range(1, n):
-        group = group + seq_parts[j]
-    total[...] = group
-    pl.loop(1, m)(lambda j: own_share(j).start())
-    own_parts[mine] = group
-
+    def columns(first, body):
+        if wide == 2:
+            pl.when(me + first + 1 < n)(functools.partial(body, 2))
+            pl.when(me + first + 1 == n)(functools.partial(body, 1))
+        else:
+            pl.when(me + first < n)(functools.partial(body, 1))
+
+    def far_column(g, first, slots):
+        count = slots * rows // HALVES
+        down, across = iotas(count)
+        lanes = pl.ds(0, count)
+        for half in range(HALVES):
+            t = (me + first) * rows + half * (rows // HALVES) + across
+            if slots == 2:
+                t = t + jnp.where(across >= rows // HALVES, rows - rows // HALVES, 0)
+            w = weight(t, me * rows + down)
+
+            def body(h, at):
+                scores = dot_nt(near(K, at), far_half(Q, first, slots, half, at))
+                pointwise(scores, w, far_col_probs.at[g, half, h, :, lanes], far_col_slope.at[g, half, h, :, lanes])
+
+            each_head(4, body)
+
+    def far_column_back(g, first, half, slots):
+        lanes = pl.ds(0, slots * rows // HALVES)
+
+        def body(h, at):
+            back = far_half(G, first, slots, half, at)
+            grad_probs = dot_nt(near(V, at), back)
+            grad_scores = (grad_probs * far_col_slope[g, half, h, :, lanes]).astype(jnp.bfloat16)
+            gk_sum[:, at] += dot_nn(grad_scores, far_half(Q, first, slots, half, at))
+            gv_sum[:, at] += dot_nn(far_col_probs[g, half, h, :, lanes], back)
+
+        each_head(4, body)
+
+    def sum_over_seq():
+        @pl.loop(1, n)
+        def _(j):
+            src = lax.rem(me + j, n)
+            pltpu.make_async_remote_copy(
+                src_ref=part, dst_ref=seq_parts.at[src],
+                send_sem=seq_send.at[j], recv_sem=seq_recv.at[src],
+                device_id={"seq": src}, device_id_type=MESH,
+            ).wait_recv()
+
+        group = seq_parts[0]
+        for j in range(1, n):
+            group = group + seq_parts[j]
+        total[...] = group
+        pl.loop(1, m)(lambda j: own_share(j).start())
+        own_parts[mine] = group
+
+    arrive_all(Q)
     for g in range(groups):
         first = 1 + g * wide
-
-        @pl.when(me + first < n)
-        def _():
+        if not relayed:
+            arrive_group(Q, first)
+        columns(first, functools.partial(far_column, g, first))
+
+    for half in range(HALVES):
+        pieces = everything[half * PIECES // HALVES : (half + 1) * PIECES // HALVES]
+        arrive_all(G, pieces)
+        if half == HALVES - 1:
+            sum_over_seq()
+        for g in range(groups):
+            first = 1 + g * wide
             if not relayed:
-                arrive_group(G, first)
-
-            def body(h, at):
-                back = far(G, first, at)
-                grad_probs = dot_nt(near(V, at), back)
-                grad_scores = (grad_probs * far_col_slope[g, h]).astype(jnp.bfloat16)
-                gk_sum[:, at] += dot_nn(grad_scores, far(Q, first, at))
-                gv_sum[:, at] += dot_nn(far_col_probs[g, h], back)
-
-            each_head(1, body)
+                arrive_group(G, first, pieces)
+            columns(first, functools.partial(far_column_back, g, first, half))
 
     results[3] = (gk_sum[...] * scale).astype(jnp.bfloat16)
     results[4] = gv_sum[...].astype(jnp.bfloat16)
@@ -468,8 +489,8 @@
             pltpu.VMEM((H, rows, rows), jnp.float32),
             pltpu.VMEM((groups, H, rows, wide * rows), jnp.bfloat16),
             pltpu.VMEM((groups, H, rows, wide * rows), jnp.float32),
-            pltpu.VMEM((groups, H, rows, wide * rows), jnp.bfloat16),
-            pltpu.VMEM((groups, H, rows, wide * rows), jnp.float32),
+            pltpu.VMEM((groups, HALVES, H, rows, wide * rows // HALVES), jnp.bfloat16),
+            pltpu.VMEM((groups, HALVES, H, rows, wide * rows // HALVES), jnp.float32),
             pltpu.VMEM((rows, width), jnp.float32),
             pltpu.VMEM((rows, width), jnp.float32),
             pltpu.VMEM((rows, width), jnp.float32),

time: 43.9 us -> 39.4 us (0.90)
  the two profiles are of different devices: /device:TPU:5 before, /device:TPU:2 now
where the time goes in v4:
time: 39.4 us; the launch traced here: 39 us
  Pallas kernels  38.3 us (97%)
  between operations  0.64 us (2%)
    pallas_call x1, Pallas kernels, per_device(): pl.pallas_call(functools.partial(kernel, n, m, reach, wide, 1.0 / math.sq...  36.2 us
    pallas_call x1, Pallas kernels, per_device(): pl.pallas_call(finish, out_shape=shapes, in_specs=[any_spec] * 6, out_spe...  2.11 us

profile of v4, /device:TPU:2, one launch (start us, length us, event | category | flops | bytes accessed | tf_op | source)
XLA Modules:
  0.0 39.0 jit_solution(10614841607633355346)
XLA Ops:
  0.6 36.2 %shard_map.118 = (bf16[1,128,1024]{2,1,0:T(8,128)(2,1)}, bf16[1,128,1024]{2,1,0:T(8,128)(2,1)}, bf16[1,128,1024]{2,1,0:T(8,128)(2,1)}, bf16[1,128,1024]{2,1,0:T(...) custom-call(s32[1,4]{1,0:T(1,128)} %lens_hbm.1, f32[1,1024]{1,0:T(1,128)} %bitcast.2, ...), custom_call_target="tpu_custom_call" | custom-call | flops 805306368 | bytes 2621440 | tf_op jit(solution)/shard_map/pallas_call | solution.py:475
  36.9 2.1 %shard_map.119 = (bf16[1,128,1024]{2,1,0:T(8,128)(2,1)}, bf16[1,128,1024]{2,1,0:T(8,128)(2,1)}, bf16[1,128,1024]{2,1,0:T(8,128)(2,1)}, bf16[1,128,1024]{2,1,0:T(...) custom-call(bf16[1,128,1024]{2,1,0:T(8,128)(2,1)} %get-tuple-element.18.refs_0_, ...), custom_call_target="tpu_custom_call" | custom-call | tf_op jit(solution)/shard_map/pallas_call | solution.py:514

commit v5 on v4

--- a/solution.py
+++ b/solution.py
@@ -162,18 +162,13 @@
             pl.when(me != relayer)(functools.partial(arrive_group, what, 1, pieces))
 
     start(K, everything)
-    start(V, everything)
     if relayed:
-        pl.when(me != 3)(functools.partial(start, Q, everything))
-
         @pl.when(me == 3)
         def _():
             for c in everything:
                 send(Q, 2, c).start()
             for c in everything[: PIECES // 2]:
                 send(Q, 1, c).start()
-    else:
-        start(Q, everything)
 
     if wide == 2:
         for d in range(2, reach + 1, 2):
@@ -223,6 +218,13 @@
 
     each_head(4, near_column)
 
+    wait_sends(K)
+    start(V, everything)
+    if relayed:
+        pl.when(me != 3)(functools.partial(start, Q, everything))
+    else:
+        start(Q, everything)
+
     arrive_all(K)
     for g in range(groups):
         first = 1 + g * wide
@@ -247,18 +249,9 @@
         def _():
             for c in everything[PIECES // 2 :]:
                 send(Q, 1, c).start()
-    for g in range(groups):
-        first = 1 + g * wide
-
-        @pl.when(me >= first)
-        def _():
-            if not relayed:
-                arrive_group(V, first)
-
-            def body(h, at):
-                attended[:, at] += dot_nn(far_row_probs[g, h], far(V, first, at))
-
-            each_head(4, body)
+    if not relayed:
+        for g in range(groups):
+            arrive_group(V, 1 + g * wide)
 
     for copy in loads[3:5]:
         copy.wait()
@@ -267,6 +260,18 @@
 
     @pl.loop(0, HALVES)
     def _(half):
+        length = rows // HALVES
+        part_rows = pl.ds(pl.multiple_of(half * length, length), length)
+        for g in range(groups):
+            first = 1 + g * wide
+
+            @pl.when(me >= first)
+            def _():
+                def body(h, at):
+                    attended[part_rows, at] += dot_nn(far_row_probs[g, h, part_rows, :], far(V, first, at))
+
+                each_head(H, body)
+
         pieces = [half * (PIECES // HALVES) + c for c in range(PIECES // HALVES)]
         for c in pieces:
             at = span(c)
@@ -435,7 +440,8 @@
     last.start()
 
     for what in (K, V, Q, G):
-        wait_sends(what)
+        if what != K:
+            wait_sends(what)
         if relayed:
             @pl.when(me == (3 if later(what) else 0))
             def _():

time: 39.4 us -> 39.6 us (level)
  no operation moved by 1% of the time
where the time goes in v5:
time: 39.6 us; the launch traced here: 39.2 us
  Pallas kernels  38.6 us (97%)
  between operations  0.64 us (2%)
    pallas_call x1, Pallas kernels, per_device(): pl.pallas_call(functools.partial(kernel, n, m, reach, wide, 1.0 / math.sq...  36.5 us
    pallas_call x1, Pallas kernels, per_device(): pl.pallas_call(finish, out_shape=shapes, in_specs=[any_spec] * 6, out_spe...  2.11 us

profile of v5, /device:TPU:2, one launch (start us, length us, event | category | flops | bytes accessed | tf_op | source)
XLA Modules:
  0.0 39.2 jit_solution(6681517660779762811)
XLA Ops:
  0.6 36.5 %shard_map.118 = (bf16[1,128,1024]{2,1,0:T(8,128)(2,1)}, bf16[1,128,1024]{2,1,0:T(8,128)(2,1)}, bf16[1,128,1024]{2,1,0:T(8,128)(2,1)}, bf16[1,128,1024]{2,1,0:T(...) custom-call(s32[1,4]{1,0:T(1,128)} %lens_hbm.1, f32[1,1024]{1,0:T(1,128)} %bitcast.2, ...), custom_call_target="tpu_custom_call" | custom-call | flops 805306368 | bytes 2621440 | tf_op jit(solution)/shard_map/pallas_call | solution.py:481
  37.1 2.1 %shard_map.119 = (bf16[1,128,1024]{2,1,0:T(8,128)(2,1)}, bf16[1,128,1024]{2,1,0:T(8,128)(2,1)}, bf16[1,128,1024]{2,1,0:T(8,128)(2,1)}, bf16[1,128,1024]{2,1,0:T(...) custom-call(bf16[1,128,1024]{2,1,0:T(8,128)(2,1)} %get-tuple-element.18.refs_0_, ...), custom_call_target="tpu_custom_call" | custom-call | tf_op jit(solution)/shard_map/pallas_call | solution.py:520

commit v6 on v5

--- a/solution.py
+++ b/solution.py
@@ -11,7 +11,7 @@
 H = 8
 MESH = pl.DeviceIdType.MESH
 K, V, Q, G = 0, 1, 2, 3
-PIECES = 4
+PIECES = 8
 HALVES = 2
 ROOM = 60 * 1024 * 1024
 
@@ -162,6 +162,11 @@
             pl.when(me != relayer)(functools.partial(arrive_group, what, 1, pieces))
 
     start(K, everything)
+    start(V, everything)
+    if relayed:
+        pl.when(me != 3)(functools.partial(start, Q, everything))
+    else:
+        start(Q, everything)
     if relayed:
         @pl.when(me == 3)
         def _():
@@ -218,13 +223,6 @@
 
     each_head(4, near_column)
 
-    wait_sends(K)
-    start(V, everything)
-    if relayed:
-        pl.when(me != 3)(functools.partial(start, Q, everything))
-    else:
-        start(Q, everything)
-
     arrive_all(K)
     for g in range(groups):
         first = 1 + g * wide
@@ -256,7 +254,7 @@
     for copy in loads[3:5]:
         copy.wait()
     gain = gain_ref[...]
-    step = piece
+    step = 32 if rows % 32 == 0 else rows
 
     @pl.loop(0, HALVES)
     def _(half):
@@ -378,8 +376,14 @@
             back = far_half(G, first, slots, half, at)
             grad_probs = dot_nt(near(V, at), back)
             grad_scores = (grad_probs * far_col_slope[g, half, h, :, lanes]).astype(jnp.bfloat16)
-            gk_sum[:, at] += dot_nn(grad_scores, far_half(Q, first, slots, half, at))
-            gv_sum[:, at] += dot_nn(far_col_probs[g, half, h, :, lanes], back)
+            key_sum = gk_sum[:, at] + dot_nn(grad_scores, far_half(Q, first, slots, half, at))
+            value_sum = gv_sum[:, at] + dot_nn(far_col_probs[g, half, h, :, lanes], back)
+            if groups == 1 and half == HALVES - 1:
+                results[3, :, at] = (key_sum * scale).astype(jnp.bfloat16)
+                results[4, :, at] = value_sum.astype(jnp.bfloat16)
+            else:
+                gk_sum[:, at] = key_sum
+                gv_sum[:, at] = value_sum
 
         each_head(4, body)
 
@@ -400,6 +404,7 @@
         pl.loop(1, m)(lambda j: own_share(j).start())
         own_parts[mine] = group
 
+    wait_sends(V)
     arrive_all(Q)
     for g in range(groups):
         first = 1 + g * wide
@@ -410,7 +415,7 @@
     for half in range(HALVES):
         pieces = everything[half * PIECES // HALVES : (half + 1) * PIECES // HALVES]
         arrive_all(G, pieces)
-        if half == HALVES - 1:
+        if half == 0:
             sum_over_seq()
         for g in range(groups):
             first = 1 + g * wide
@@ -418,8 +423,11 @@
                 arrive_group(G, first, pieces)
             columns(first, functools.partial(far_column_back, g, first, half))
 
-    results[3] = (gk_sum[...] * scale).astype(jnp.bfloat16)
-    results[4] = gv_sum[...].astype(jnp.bfloat16)
+    @pl.when((me == n - 1) | (groups > 1))
+    def _():
+        results[3] = (gk_sum[...] * scale).astype(jnp.bfloat16)
+        results[4] = gv_sum[...].astype(jnp.bfloat16)
+
     stores[3].start()
     stores[4].start()
 
@@ -440,7 +448,7 @@
     last.start()
 
     for what in (K, V, Q, G):
-        if what != K:
+        if what != V:
             wait_sends(what)
         if relayed:
             @pl.when(me == (3 if later(what) else 0))

time: 39.6 us -> 41 us (1.035)
  Pallas kernels: 38.6 us -> 40.1 us
    pallas_call x1, Pallas kernels: 36.5 us -> 38 us  [per_device(): pl.pallas_call(functools.partial(kernel, n, m, reach, wide, 1.0 / math.sq...]
where the time goes in v6:
time: 41 us; the launch traced here: 40.8 us
  Pallas kernels  40.1 us (98%)
  between operations  0.64 us (2%)
    pallas_call x1, Pallas kernels, per_device(): pl.pallas_call(functools.partial(kernel, n, m, reach, wide, 1.0 / math.sq...  38 us
    pallas_call x1, Pallas kernels, per_device(): pl.pallas_call(finish, out_shape=shapes, in_specs=[any_spec] * 6, out_spe...  2.11 us

profile of v6, /device:TPU:2, one launch (start us, length us, event | category | flops | bytes accessed | tf_op | source)
XLA Modules:
  0.0 40.8 jit_solution(15727648147312864507)
XLA Ops:
  0.6 38.0 %shard_map.118 = (bf16[1,128,1024]{2,1,0:T(8,128)(2,1)}, bf16[1,128,1024]{2,1,0:T(8,128)(2,1)}, bf16[1,128,1024]{2,1,0:T(8,128)(2,1)}, bf16[1,128,1024]{2,1,0:T(...) custom-call(s32[1,4]{1,0:T(1,128)} %lens_hbm.1, f32[1,1024]{1,0:T(1,128)} %bitcast.2, ...), custom_call_target="tpu_custom_call" | custom-call | flops 805306368 | bytes 2621440 | tf_op jit(solution)/shard_map/pallas_call | solution.py:489
  38.7 2.1 %shard_map.119 = (bf16[1,128,1024]{2,1,0:T(8,128)(2,1)}, bf16[1,128,1024]{2,1,0:T(8,128)(2,1)}, bf16[1,128,1024]{2,1,0:T(8,128)(2,1)}, bf16[1,128,1024]{2,1,0:T(...) custom-call(bf16[1,128,1024]{2,1,0:T(8,128)(2,1)} %get-tuple-element.18.refs_0_, ...), custom_call_target="tpu_custom_call" | custom-call | tf_op jit(solution)/shard_map/pallas_call | solution.py:528

commit v7 on v6

--- a/solution.py
+++ b/solution.py
@@ -11,7 +11,7 @@
 H = 8
 MESH = pl.DeviceIdType.MESH
 K, V, Q, G = 0, 1, 2, 3
-PIECES = 8
+PIECES = 2
 HALVES = 2
 ROOM = 60 * 1024 * 1024
 
@@ -254,7 +254,7 @@
     for copy in loads[3:5]:
         copy.wait()
     gain = gain_ref[...]
-    step = 32 if rows % 32 == 0 else rows
+    step = math.gcd(32, rows // HALVES)
 
     @pl.loop(0, HALVES)
     def _(half):
@@ -271,8 +271,8 @@
                 each_head(H, body)
 
         pieces = [half * (PIECES // HALVES) + c for c in range(PIECES // HALVES)]
-        for c in pieces:
-            at = span(c)
+        for r in range(0, length, step):
+            at = pl.ds(pl.multiple_of(half * length + r, step), step)
             att = attended[at, :]
             center = att - jnp.mean(att, axis=1, keepdims=True)
             rstd = lax.rsqrt(jnp.mean(center * center, axis=1, keepdims=True) + 1e-05)

time: 41 us -> 40.5 us (0.988)
  no operation moved by 1% of the time
where the time goes in v7:
time: 40.5 us; the launch traced here: 40.4 us
  Pallas kernels  39.7 us (98%)
  between operations  0.64 us (2%)
    pallas_call x1, Pallas kernels, per_device(): pl.pallas_call(functools.partial(kernel, n, m, reach, wide, 1.0 / math.sq...  37.6 us
    pallas_call x1, Pallas kernels, per_device(): pl.pallas_call(finish, out_shape=shapes, in_specs=[any_spec] * 6, out_spe...  2.11 us

profile of v7, /device:TPU:2, one launch (start us, length us, event | category | flops | bytes accessed | tf_op | source)
XLA Modules:
  0.0 40.4 jit_solution(7650200539298740906)
XLA Ops:
  0.6 37.6 %shard_map.118 = (bf16[1,128,1024]{2,1,0:T(8,128)(2,1)}, bf16[1,128,1024]{2,1,0:T(8,128)(2,1)}, bf16[1,128,1024]{2,1,0:T(8,128)(2,1)}, bf16[1,128,1024]{2,1,0:T(...) custom-call(s32[1,4]{1,0:T(1,128)} %lens_hbm.1, f32[1,1024]{1,0:T(1,128)} %bitcast.2, ...), custom_call_target="tpu_custom_call" | custom-call | flops 805306368 | bytes 2621440 | tf_op jit(solution)/shard_map/pallas_call | solution.py:489
  38.3 2.1 %shard_map.119 = (bf16[1,128,1024]{2,1,0:T(8,128)(2,1)}, bf16[1,128,1024]{2,1,0:T(8,128)(2,1)}, bf16[1,128,1024]{2,1,0:T(8,128)(2,1)}, bf16[1,128,1024]{2,1,0:T(...) custom-call(bf16[1,128,1024]{2,1,0:T(8,128)(2,1)} %get-tuple-element.18.refs_0_, ...), custom_call_target="tpu_custom_call" | custom-call | tf_op jit(solution)/shard_map/pallas_call | solution.py:528

commit v8 on v4

--- a/solution.py
+++ b/solution.py
@@ -373,8 +373,14 @@
             back = far_half(G, first, slots, half, at)
             grad_probs = dot_nt(near(V, at), back)
             grad_scores = (grad_probs * far_col_slope[g, half, h, :, lanes]).astype(jnp.bfloat16)
-            gk_sum[:, at] += dot_nn(grad_scores, far_half(Q, first, slots, half, at))
-            gv_sum[:, at] += dot_nn(far_col_probs[g, half, h, :, lanes], back)
+            key_sum = gk_sum[:, at] + dot_nn(grad_scores, far_half(Q, first, slots, half, at))
+            value_sum = gv_sum[:, at] + dot_nn(far_col_probs[g, half, h, :, lanes], back)
+            if groups == 1 and half == HALVES - 1:
+                results[3, :, at] = (key_sum * scale).astype(jnp.bfloat16)
+                results[4, :, at] = value_sum.astype(jnp.bfloat16)
+            else:
+                gk_sum[:, at] = key_sum
+                gv_sum[:, at] = value_sum
 
         each_head(4, body)
 
@@ -405,7 +411,7 @@
     for half in range(HALVES):
         pieces = everything[half * PIECES // HALVES : (half + 1) * PIECES // HALVES]
         arrive_all(G, pieces)
-        if half == HALVES - 1:
+        if half == 0:
             sum_over_seq()
         for g in range(groups):
             first = 1 + g * wide
@@ -413,8 +419,11 @@
                 arrive_group(G, first, pieces)
             columns(first, functools.partial(far_column_back, g, first, half))
 
-    results[3] = (gk_sum[...] * scale).astype(jnp.bfloat16)
-    results[4] = gv_sum[...].astype(jnp.bfloat16)
+    @pl.when((me == n - 1) | (groups > 1))
+    def _():
+        results[3] = (gk_sum[...] * scale).astype(jnp.bfloat16)
+        results[4] = gv_sum[...].astype(jnp.bfloat16)
+
     stores[3].start()
     stores[4].start()
 

time: 39.4 us -> 40.2 us (1.020)
  Pallas kernels: 38.3 us -> 39.4 us
    pallas_call x1, Pallas kernels: 36.2 us -> 37.3 us  [per_device(): pl.pallas_call(functools.partial(kernel, n, m, reach, wide, 1.0 / math.sq...]
where the time goes in v8:
time: 40.2 us; the launch traced here: 40.1 us
  Pallas kernels  39.4 us (98%)
  between operations  0.64 us (2%)
    pallas_call x1, Pallas kernels, per_device(): pl.pallas_call(functools.partial(kernel, n, m, reach, wide, 1.0 / math.sq...  37.3 us
    pallas_call x1, Pallas kernels, per_device(): pl.pallas_call(finish, out_shape=shapes, in_specs=[any_spec] * 6, out_spe...  2.11 us

profile of v8, /device:TPU:2, one launch (start us, length us, event | category | flops | bytes accessed | tf_op | source)
XLA Modules:
  0.0 40.1 jit_solution(5881508621081197909)
XLA Ops:
  0.6 37.3 %shard_map.118 = (bf16[1,128,1024]{2,1,0:T(8,128)(2,1)}, bf16[1,128,1024]{2,1,0:T(8,128)(2,1)}, bf16[1,128,1024]{2,1,0:T(8,128)(2,1)}, bf16[1,128,1024]{2,1,0:T(...) custom-call(s32[1,4]{1,0:T(1,128)} %lens_hbm.1, f32[1,1024]{1,0:T(1,128)} %bitcast.2, ...), custom_call_target="tpu_custom_call" | custom-call | flops 805306368 | bytes 2621440 | tf_op jit(solution)/shard_map/pallas_call | solution.py:484
  38.0 2.1 %shard_map.119 = (bf16[1,128,1024]{2,1,0:T(8,128)(2,1)}, bf16[1,128,1024]{2,1,0:T(8,128)(2,1)}, bf16[1,128,1024]{2,1,0:T(8,128)(2,1)}, bf16[1,128,1024]{2,1,0:T(...) custom-call(bf16[1,128,1024]{2,1,0:T(8,128)(2,1)} %get-tuple-element.18.refs_0_, ...), custom_call_target="tpu_custom_call" | custom-call | tf_op jit(solution)/shard_map/pallas_call | solution.py:523
